TPU v7x, 128 devices: a whole 4x4x4 slice. The times are simulated.
128 devices in a mesh: dap: 128 (over z, y, x, core).
Axes of the slice: x: 4, y: 4, z: 4, core: 2. Of those that a mesh axis runs over, the one named last changes fastest.
Arguments:
- pair: bfloat16 [512, 512, 128], P('dap'), may hold values from -6 to 6
- pair_mask: int32 [512, 512], P('dap'), may hold values 0 or 1
- norm_gains: float32 [3, 128], replicated, may hold values from 0.25 to 1.75
- w_edges: bfloat16 [128, 512], replicated, may hold values from -0.5 to 0.5
- w_tri_gate: bfloat16 [128, 128], replicated, may hold values from -0.5 to 0.5
- w_tri_out: bfloat16 [128, 128], replicated, may hold values from -0.5 to 0.5
- w_attn_in: bfloat16 [128, 512], replicated, may hold values from -0.5 to 0.5
- w_tri_bias: bfloat16 [128, 4], replicated, may hold values from -0.5 to 0.5
- w_attn_out: bfloat16 [128, 128], replicated, may hold values from -0.5 to 0.5
Outputs:
- updated: bfloat16 [512, 512, 128], P('dap')
All inputs are finite; a program needn't handle non-finite values. No bound on the sum of `pair_mask` on one device may be relied on, other than what follows from the above.
Results may differ from a plain program's by a relative error of at most 0.013.
Values may be sent and summed in bfloat16 or wider, within the bound.
No kernel may reach another device: no remote copies, remote signals or barrier semaphores. Data moves between devices by JAX's collectives and lax.ppermute only.
A program may use at most 256 MiB of HBM per device.

v0:
```python
import jax
import jax.numpy as jnp
from jax import lax
from jax.sharding import PartitionSpec as P


def layer_norm(values, gain):
    mean = jnp.mean(values, axis=-1, keepdims=True)
    centered = values - mean
    var = jnp.mean(centered * centered, axis=-1, keepdims=True)
    return centered / jnp.sqrt(var + 1e-05) * gain


def per_device(
    pair, pair_mask, norm_gains, w_edges, w_tri_gate, w_tri_out, w_attn_in, w_tri_bias, w_attn_out
):
    total = pair.shape[1]
    hidden = w_tri_out.shape[0]
    heads = w_tri_bias.shape[1]
    width = w_attn_out.shape[0]
    head_dim = width // heads
    pair_f = pair.astype(jnp.float32)
    normed = layer_norm(pair_f, norm_gains[0]).astype(jnp.bfloat16)
    edges = jnp.einsum("ijc,cd->ijd", normed, w_edges, preferred_element_type=jnp.float32)
    mask_f = pair_mask.astype(jnp.float32)[:, :, None]
    left = (
        mask_f * jax.nn.sigmoid(edges[:, :, 0:hidden]) * edges[:, :, hidden : 2 * hidden]
    ).astype(jnp.bfloat16)
    right = (
        mask_f
        * jax.nn.sigmoid(edges[:, :, 2 * hidden : 3 * hidden])
        * edges[:, :, 3 * hidden : 4 * hidden]
    ).astype(jnp.bfloat16)
    gathered = lax.all_gather(right, "dap", axis=0, tiled=True)
    product = jnp.einsum("ikc,jkc->ijc", left, gathered, preferred_element_type=jnp.float32)
    prod_normed = layer_norm(product, norm_gains[1]).astype(jnp.bfloat16)
    gate = jax.nn.sigmoid(
        jnp.einsum("ijc,cd->ijd", normed, w_tri_gate, preferred_element_type=jnp.float32)
    )
    update = gate * jnp.einsum(
        "ijc,cd->ijd", prod_normed, w_tri_out, preferred_element_type=jnp.float32
    )
    pair_mid = (pair_f + update).astype(jnp.bfloat16)
    mid_f = pair_mid.astype(jnp.float32)
    mid_normed = layer_norm(mid_f, norm_gains[2]).astype(jnp.bfloat16)
    own_bias = jnp.einsum(
        "jkc,ch->hjk", mid_normed, w_tri_bias, preferred_element_type=jnp.float32
    ).astype(jnp.bfloat16)
    tri_bias = lax.all_gather(own_bias, "dap", axis=1, tiled=True)
    bias_f = tri_bias.astype(jnp.float32)
    scale = jnp.sqrt(jnp.float32(head_dim))

    def attend_row(inputs):
        normed_row, mask_row, mid_row = inputs
        packed = jnp.dot(normed_row, w_attn_in, preferred_element_type=jnp.float32)
        query = packed[:, 0:width].astype(jnp.bfloat16).reshape(total, heads, head_dim)
        key = packed[:, width : 2 * width].astype(jnp.bfloat16).reshape(total, heads, head_dim)
        value = (
            packed[:, 2 * width : 3 * width].astype(jnp.bfloat16).reshape(total, heads, head_dim)
        )
        att_gate = jax.nn.sigmoid(packed[:, 3 * width : 4 * width])
        logits = jnp.einsum("jhd,khd->hjk", query, key, preferred_element_type=jnp.float32) / scale
        logits = (
            logits + bias_f + 1000000000.0 * (mask_row.astype(jnp.float32)[None, None, :] - 1.0)
        )
        top = jnp.max(logits, axis=-1, keepdims=True)
        expo = jnp.exp(logits - top)
        weights = (expo / jnp.sum(expo, axis=-1, keepdims=True)).astype(jnp.bfloat16)
        mixed = jnp.einsum(
            "hjk,khd->jhd", weights, value, preferred_element_type=jnp.float32
        ).reshape(total, width)
        attended = (att_gate * mixed).astype(jnp.bfloat16)
        return (mid_row + jnp.dot(attended, w_attn_out, preferred_element_type=jnp.float32)).astype(
            jnp.bfloat16
        )

    return lax.map(attend_row, (mid_normed, pair_mask, mid_f))


def solution(mesh):
    placed = (P("dap", None, None), P("dap", None), P(), P(), P(), P(), P(), P(), P())
    return jax.shard_map(
        per_device, mesh=mesh, in_specs=placed, out_specs=P("dap", None, None), check_vma=False
    )
```

profile of v0, /device:TPU:1, one launch (start us, length us, event | category | flops | bytes accessed | tf_op | source)
XLA Modules:
  0.0 424.7 jit_solution(9802473907473933949)
XLA Ops:
  6.5 1.3 copy.28
  8.1 0.8 slice_bitcast_fusion
  9.6 0.8 fusion.40
  11.1 1.0 copy.34
  12.2 168.4 %all-gather.3.cloned.1.call-done = bf16[512,512,128]{2,1,0:T(8,128)(2,1)} async-done(((bf16[4,512,128]{2,1,0:T(8,128)(2,1)}), bf16[512,512,128]{2,1,0:T(8,128)(2,1)}) %all-gather.3.cloned.1.call-update) | async-done | bytes 67108880 | tf_op jit(solution)/shard_map/all_gather | solution.py:34
  180.6 88.9 %copy.37 = bf16[512,512,128]{1,0,2:T(8,128)(2,1)} copy(bf16[512,512,128]{2,1,0:T(8,128)(2,1)} %all-gather.3.cloned.1.call-done) | data formatting | bytes 134217728 | tf_op jit(solution)/shard_map/all_gather | solution.py:34
  269.5 25.5 %fusion.50 = (f32[4,512]{1,0:T(4,128)S(1)}, f32[4,512,128]{1,0,2:T(4,128)S(1)}) fusion(bf16[512,512,128]{1,0,2:T(8,128)(2,1)} %copy.37, bf16[4,512,128]{1,2,0:T(8,128)(2,1)S(1)} %get-tuple-element.144), kind=kOutput, calls=%fused_computation.78 | convolution fusion | flops 268695552 | bytes 68689920 | tf_op jit(solution)/shard_map/ikc,jkc->ijc/dot_general | solution.py:35
  297.0 0.8 fusion.23
  297.8 64.6 %all-gather.5.cloned.1.call-done = bf16[4,512,512]{2,0,1:T(4,128)(2,1)} async-done(((bf16[4,4,512]{2,0,1:T(4,128)(2,1)}), bf16[4,512,512]{2,0,1:T(4,128)(2,1)}) %all-gather.5.cloned.1.call-update) | async-done | bytes 2097168 | tf_op jit(solution)/shard_map/all_gather | solution.py:49
  362.4 4.8 %copy.44 = f32[4,512,512]{1,2,0:T(8,128)} copy(bf16[4,512,512]{2,0,1:T(4,128)(2,1)} %all-gather.5.cloned.1.call-done) | data formatting | bytes 6291456 | tf_op jit(solution)/shard_map/while | solution.py:77
  367.3 50.6 %while.12 = (s32[]{:T(128)}, bf16[4,512,128]{2,1,0:T(8,128)(2,1)}, f32[4,512,128]{1,2,0:T(8,128)S(1)}, bf16[4,512,128]{1,2,0:T(8,128)(2,1)S(1)}, bf16[128,512]{1...) while((s32[]{:T(128)}, bf16[4,512,128]{2,1,0:T(8,128)(2,1)}, ...), condition=%wide.region_9.10_spmd, body=%wide.region_6.9_spmd.sunk | while | flops 227217920 | bytes 39115396 | solution.py:77
  367.6 0.7 add_multiply_fusion.2
  368.4 3.1 add_add_fusion.2
  371.4 2.0 copy-done.1
  373.4 0.8 fusion.86
  374.2 4.6 %fusion.87 = f32[4,32,512]{2,1,0:T(8,128)S(1)} fusion(bf16[512,4,32]{0,2,1:T(8,128)(2,1)S(1)} %bitcast.90, f32[4,512]{1,0:T(4,128)S(1)} %fusion.86, f32[4,512,512]{1,2,0:T(8,128)} %copy-done.1), kind=kOutput, calls=%fused_computation.4.clone.1 | convolution fusion | flops 70257152 | bytes 4595712 | tf_op jit(solution)/shard_map/while/body/eval_jaxpr/hjk,khd->jhd/dot_general | solution.py:69
  379.0 0.9 fusion.89
  381.0 3.1 add_add_fusion.2
  384.1 2.0 copy-done.1
  386.0 0.8 fusion.86
  386.9 4.6 %fusion.87 = f32[4,32,512]{2,1,0:T(8,128)S(1)} fusion(bf16[512,4,32]{0,2,1:T(8,128)(2,1)S(1)} %bitcast.90, f32[4,512]{1,0:T(4,128)S(1)} %fusion.86, f32[4,512,512]{1,2,0:T(8,128)} %copy-done.1), kind=kOutput, calls=%fused_computation.4.clone.1 | convolution fusion | flops 70257152 | bytes 4595712 | tf_op jit(solution)/shard_map/while/body/eval_jaxpr/hjk,khd->jhd/dot_general | solution.py:69
  391.7 0.9 fusion.89
  393.6 3.1 add_add_fusion.2
  396.7 2.0 copy-done.1
  398.7 0.8 fusion.86
  399.5 4.6 %fusion.87 = f32[4,32,512]{2,1,0:T(8,128)S(1)} fusion(bf16[512,4,32]{0,2,1:T(8,128)(2,1)S(1)} %bitcast.90, f32[4,512]{1,0:T(4,128)S(1)} %fusion.86, f32[4,512,512]{1,2,0:T(8,128)} %copy-done.1), kind=kOutput, calls=%fused_computation.4.clone.1 | convolution fusion | flops 70257152 | bytes 4595712 | tf_op jit(solution)/shard_map/while/body/eval_jaxpr/hjk,khd->jhd/dot_general | solution.py:69
  404.3 0.9 fusion.89
  406.3 3.1 add_add_fusion.2
  409.4 2.0 copy-done.1
  411.3 0.8 fusion.86
  412.1 4.6 %fusion.87 = f32[4,32,512]{2,1,0:T(8,128)S(1)} fusion(bf16[512,4,32]{0,2,1:T(8,128)(2,1)S(1)} %bitcast.90, f32[4,512]{1,0:T(4,128)S(1)} %fusion.86, f32[4,512,512]{1,2,0:T(8,128)} %copy-done.1), kind=kOutput, calls=%fused_computation.4.clone.1 | convolution fusion | flops 70257152 | bytes 4595712 | tf_op jit(solution)/shard_map/while/body/eval_jaxpr/hjk,khd->jhd/dot_general | solution.py:69
  416.9 0.9 fusion.89
  (60 shorter events, 8.2 us)
Async XLA Ops:
  6.5 3.1 copy-start
  6.5 174.0 %all-gather.3.cloned.1.call-start = ((), (), s32[]{:S(2)}) async-start(), calls=%async_computation | async-start | bytes 67633152 | tf_op jit(solution)/shard_map/all_gather | solution.py:34
  12.1 350.3 %all-gather.5.cloned.1.call-start = ((), (), s32[]{:S(2)}) async-start(), calls=%async_computation.1 | async-start | bytes 2113536 | tf_op jit(solution)/shard_map/all_gather | solution.py:49
  269.5 26.2 %copy-start.4 = (bf16[128,128]{1,0:T(8,128)(2,1)S(1)}, bf16[128,128]{1,0:T(8,128)(2,1)}, u32[]{:S(2)}) copy-start(bf16[128,128]{1,0:T(8,128)(2,1)} %param.16) | copy-start | bytes 98308
  294.9 1.1 copy-start.6
  296.0 1.0 copy-start.5
  296.8 70.4 %copy-start.2 = (bf16[128,512]{1,0:T(8,128)(2,1)S(1)}, bf16[128,512]{1,0:T(8,128)(2,1)}, u32[]{:S(2)}) copy-start(bf16[128,512]{1,0:T(8,128)(2,1)} %param.17) | copy-start | bytes 393220
  296.8 70.4 %copy-start.3 = (bf16[128,128]{1,0:T(8,128)(2,1)S(1)}, bf16[128,128]{1,0:T(8,128)(2,1)}, u32[]{:S(2)}) copy-start(bf16[128,128]{1,0:T(8,128)(2,1)} %param.19) | copy-start | bytes 98308
  371.4 2.0 copy-start.1
  384.1 2.0 copy-start.1
  396.7 2.0 copy-start.1
  409.4 2.0 copy-start.1
Sparse Core Ops, SparseCore 0:
  12.2 168.2 all-gather.2
  297.9 64.4 all-gather.4
where the time goes:
time: 428 us; the launch traced here: 425 us
  waiting for transfers between devices  233 us (54%)
  local copies, waits for them, and re-layouts  105 us (25%)
  matrix products  63.4 us (15%)
  between operations  13.6 us (3%)
  other arithmetic  9.01 us (2%)
    all_gather x1, waiting for transfers between devices, per_device(): gathered = lax.all_gather(right, 'dap', axis=0, tiled=True)  168 us
    all_gather x1, local copies, waits for them, and re-layouts, per_device(): gathered = lax.all_gather(right, 'dap', axis=0, tiled=True)  88.9 us
    all_gather x1, waiting for transfers between devices, per_device(): tri_bias = lax.all_gather(own_bias, 'dap', axis=1, tiled=True)  64.6 us
    dot_general x1, matrix products, per_device(): jnp.einsum('ikc,jkc->ijc', left, gathered, preferred_element_type=jnp.flo...  25.5 us
    dot_general x4, matrix products, attend_row(): jnp.einsum('hjk,khd->jhd', weights, value, preferred_element_type=jnp.flo...  18.2 us
    dot_general x4, matrix products, attend_row(): jnp.einsum('jhd,khd->hjk', query, key, preferred_element_type=jnp.float32)  12.3 us
  transfers between devices with their start and end apart: 2, of which 2 were waited for; matrix products, arithmetic and copies ran while one was open for 0% of the time, Pallas kernels for 0%

commit v1 on v0

v1 whole, which is shorter than its diff:
```python
import functools
import math

import jax
import jax.numpy as jnp
from jax import lax
from jax.experimental import pallas as pl
from jax.experimental.pallas import tpu as pltpu
from jax.sharding import PartitionSpec as P

F32 = jnp.float32
BF16 = jnp.bfloat16
VMEM_LIMIT = 48 * 1024 * 1024
LOG2E = math.log2(math.e)


def dot(a, b, ca, cb):
    return lax.dot_general(a, b, (((ca,), (cb,)), ((), ())), preferred_element_type=F32)


def norm_rows(values, gain):
    mean = jnp.mean(values, axis=-1, keepdims=True)
    centered = values - mean
    var = jnp.mean(centered * centered, axis=-1, keepdims=True)
    return centered * lax.rsqrt(var + 1e-05) * gain


def edges_kernel(pair_ref, mask_ref, gains_ref, w_ref, out_ref):
    row = pl.program_id(0)
    hidden = out_ref.shape[0]
    normed = norm_rows(pair_ref[...].astype(F32), gains_ref[0:1, :]).astype(BF16)
    edges = dot(w_ref[...], normed, 0, 1)
    mask = mask_ref[pl.ds(row, 1), :].astype(F32)
    for side in range(2):
        gate = edges[2 * side * hidden : (2 * side + 1) * hidden]
        value = edges[(2 * side + 1) * hidden : (2 * side + 2) * hidden]
        out_ref[:, side, :] = (mask * jax.nn.sigmoid(gate) * value).astype(BF16)


def product_kernel(left_ref, right_ref, out_ref):
    total = right_ref.shape[0]
    for row in range(left_ref.shape[1] // total):
        cols = slice(row * total, (row + 1) * total)
        out_ref[:, cols] = dot(left_ref[:, cols], right_ref[...], 1, 1).astype(BF16)


def middle_kernel(prod_ref, pair_ref, gains_ref, wg_ref, wo_ref, wb_ref, mid_ref, normed_ref, bias_ref):
    prod = prod_ref[...].astype(F32)
    mean = jnp.mean(prod, axis=0, keepdims=True)
    centered = prod - mean
    var = jnp.mean(centered * centered, axis=0, keepdims=True)
    prod_normed = (centered * lax.rsqrt(var + 1e-05) * gains_ref[1:2, :].T).astype(BF16)
    pair = pair_ref[...].astype(F32)
    normed = norm_rows(pair, gains_ref[0:1, :]).astype(BF16)
    gate = jax.nn.sigmoid(dot(normed, wg_ref[...], 1, 0))
    mid = (pair + gate * dot(prod_normed, wo_ref[...], 0, 0)).astype(BF16)
    mid_ref[...] = mid
    mid_normed = norm_rows(mid.astype(F32), gains_ref[2:3, :]).astype(BF16)
    normed_ref[...] = mid_normed
    bias_ref[...] = dot(wb_ref[...], mid_normed, 0, 1).astype(BF16)


def attention_kernel(head_dim, normed_ref, mid_ref, mask_ref, bias_ref, win_ref, wout_ref, out_ref):
    row = pl.program_id(0)
    heads = bias_ref.shape[0]
    total, width = normed_ref.shape
    packed = dot(normed_ref[...], win_ref[...], 1, 0)
    query = packed[:, 0:width].astype(BF16)
    key = packed[:, width : 2 * width].astype(BF16)
    value = packed[:, 2 * width : 3 * width].astype(BF16)
    lane_head = lax.broadcasted_iota(jnp.int32, (1, width), 1) // head_dim
    mask = 1000000000.0 * (mask_ref[pl.ds(row, 1), :].astype(F32) - 1.0)
    scale = 1.0 / math.sqrt(head_dim)
    mixed = jnp.zeros((total, 2 * width), F32)
    for head in range(heads):
        pick = (lane_head == head).astype(BF16)
        logits = dot(query * pick, key, 1, 1) * scale + bias_ref[head].astype(F32) + mask
        top = jnp.max(logits, axis=-1, keepdims=True)
        expo = jnp.exp(logits - top).astype(BF16)
        both = jnp.concatenate([value * pick, jnp.broadcast_to(pick, value.shape)], axis=1)
        mixed = mixed + dot(expo, both, 1, 0)
    att_gate = jax.nn.sigmoid(packed[:, 3 * width : 4 * width])
    attended = (att_gate * mixed[:, :width] / mixed[:, width:]).astype(BF16)
    update = dot(attended, wout_ref[...], 1, 0)
    out_ref[...] = (mid_ref[...].astype(F32) + update).astype(BF16)


def params():
    return pltpu.CompilerParams(vmem_limit_bytes=VMEM_LIMIT)


def whole(array):
    return pl.BlockSpec(array.shape, lambda *_: (0,) * array.ndim)


def exchange(array):
    return lax.all_to_all(array, "dap", 0, 0, tiled=True)


def per_device(
    pair, pair_mask, norm_gains, w_edges, w_tri_gate, w_tri_out, w_attn_in, w_tri_bias, w_attn_out
):
    rows, total, width = pair.shape
    hidden = w_tri_out.shape[0]
    heads = w_tri_bias.shape[1]
    devices = total // rows
    flat = pair.reshape(rows * total, width)
    row_block = pl.BlockSpec((total, width), lambda r: (r, 0))
    sides = pl.pallas_call(
        edges_kernel,
        grid=(rows,),
        in_specs=[row_block, whole(pair_mask), whole(norm_gains), whole(w_edges)],
        out_specs=pl.BlockSpec((hidden, 2, total), lambda r: (0, 0, r)),
        out_shape=jax.ShapeDtypeStruct((hidden, 2, rows * total), BF16),
        compiler_params=params(),
    )(flat, pair_mask, norm_gains, w_edges)
    sides = exchange(sides)
    left = sides[:, 0]
    right = sides[:, 1].reshape(total, total)
    product = pl.pallas_call(
        product_kernel,
        out_shape=jax.ShapeDtypeStruct((devices, rows * total), BF16),
        compiler_params=params(),
    )(left, right)
    product = exchange(product)
    mid, mid_normed, bias = pl.pallas_call(
        middle_kernel,
        grid=(rows,),
        in_specs=[
            pl.BlockSpec((hidden, total), lambda r: (0, r)),
            row_block,
            whole(norm_gains),
            whole(w_tri_gate),
            whole(w_tri_out),
            whole(w_tri_bias),
        ],
        out_specs=[row_block, row_block, pl.BlockSpec((heads, total), lambda r: (0, r))],
        out_shape=[
            jax.ShapeDtypeStruct((rows * total, width), BF16),
            jax.ShapeDtypeStruct((rows * total, width), BF16),
            jax.ShapeDtypeStruct((heads, rows * total), BF16),
        ],
        compiler_params=params(),
    )(product, flat, norm_gains, w_tri_gate, w_tri_out, w_tri_bias)
    bias = exchange(jnp.broadcast_to(bias.reshape(1, heads, rows, total), (devices, heads, rows, total)))
    bias = bias.transpose(1, 0, 2, 3).reshape(heads, total, total)
    updated = pl.pallas_call(
        functools.partial(attention_kernel, width // heads),
        grid=(rows,),
        in_specs=[
            row_block,
            row_block,
            whole(pair_mask),
            whole(bias),
            whole(w_attn_in),
            whole(w_attn_out),
        ],
        out_specs=row_block,
        out_shape=jax.ShapeDtypeStruct((rows * total, width), BF16),
        compiler_params=params(),
    )(mid_normed, mid, pair_mask, bias, w_attn_in, w_attn_out)
    return updated.reshape(rows, total, width)


def solution(mesh):
    placed = (P("dap", None, None), P("dap", None), P(), P(), P(), P(), P(), P(), P())
    return jax.shard_map(
        per_device, mesh=mesh, in_specs=placed, out_specs=P("dap", None, None), check_vma=False
    )
```

time: 428 us -> 118 us (0.28)
  waiting for transfers between devices: 233 us -> 13.7 us
  local copies, waits for them, and re-layouts: 105 us -> 16.4 us
  blocking collectives: 0 us -> 65.5 us
  matrix products: 63.4 us -> 0 us
  Pallas kernels: 0 us -> 16.9 us
  between operations: 13.6 us -> 0.18 us
  other arithmetic: 9.01 us -> 0.99 us
  starting transfers between devices: 0.04 us -> 4.43 us
    all_gather x2 -> x0, waiting for transfers between devices: 233 us -> none  [the longest x1 168 us: per_device(): gathered = lax.all_gather(right, 'dap', axis=0, tiled=True)]
    all_gather x1 -> x0, local copies, waits for them, and re-layouts: 88.9 us -> none  [per_device(): gathered = lax.all_gather(right, 'dap', axis=0, tiled=True)]
    all_to_all x0 -> x2, blocking collectives: none -> 65.5 us  [exchange(): return lax.all_to_all(array, 'dap', 0, 0, tiled=True)]
    dot_general x21 -> x0, matrix products: 63.4 us -> none  [the longest x1 25.5 us: per_device(): jnp.einsum('ikc,jkc->ijc', left, gathered, preferred_element_type=jnp.flo...]
    pallas_call x0 -> x4, Pallas kernels: none -> 16.9 us  [the longest x1 9.81 us: per_device(): pl.pallas_call(functools.partial(attention_kernel, width // heads), grid=...]
    all_to_all x0 -> x1, waiting for transfers between devices: none -> 13.7 us  [exchange(): return lax.all_to_all(array, 'dap', 0, 0, tiled=True)]
    while x9 -> x0, local copies, waits for them, and re-layouts: 12.7 us -> none
    all_to_all x0 -> x1, starting transfers between devices: none -> 4.43 us  [exchange(): return lax.all_to_all(array, 'dap', 0, 0, tiled=True)]
  transfers between devices with their start and end apart: 2 -> 1, of which waited for: 2 -> 1; matrix products, arithmetic and copies ran while one was open for 0% -> 0% of each run, Pallas kernels for 0% -> 0%
where the time goes in v1:
time: 118 us
  blocking collectives  65.5 us (56%)
  Pallas kernels  16.9 us (14%)
  local copies, waits for them, and re-layouts  16.4 us (14%)
  waiting for transfers between devices  13.7 us (12%)
  starting transfers between devices  4.43 us (4%)
    all_to_all x2, blocking collectives, exchange(): return lax.all_to_all(array, 'dap', 0, 0, tiled=True)  65.5 us
    all_to_all x1, waiting for transfers between devices, exchange(): return lax.all_to_all(array, 'dap', 0, 0, tiled=True)  13.7 us
    pallas_call x1, Pallas kernels, per_device(): pl.pallas_call(functools.partial(attention_kernel, width // heads), grid=...  9.81 us
    unnamed x29, local copies, waits for them, and re-layouts  5.7 us
    all_to_all x1, starting transfers between devices, exchange(): return lax.all_to_all(array, 'dap', 0, 0, tiled=True)  4.43 us
    slice x1, local copies, waits for them, and re-layouts, per_device(): right = sides[:, 1].reshape(total, total)  4.13 us
    pallas_call x1, Pallas kernels, per_device(): pl.pallas_call(middle_kernel, grid=(rows,), in_specs=[pl.BlockSpec((hidde...  3.73 us
    reshape x1, local copies, waits for them, and re-layouts, per_device(): bias = bias.transpose(1, 0, 2, 3).reshape(heads, total, total)  2.58 us
  transfers between devices with their start and end apart: 1, of which 1 were waited for; matrix products, arithmetic and copies ran while one was open for 0% of the time, Pallas kernels for 0%

profile of v1, /device:TPU:1, one launch (start us, length us, event | category | flops | bytes accessed | tf_op | source)
XLA Modules:
  0.0 118.1 jit_solution(5856721615735532182)
XLA Ops:
  0.0 1.0 copy-done
  1.0 0.9 copy-done.2
  1.9 0.7 copy-done.5
  2.6 0.7 copy-done.9
  3.3 2.6 %shard_map.91 = bf16[128,2,2048]{2,1,0:T(2,128)(2,1)S(1)} custom-call(bf16[2048,128]{1,0:T(8,128)(2,1)S(1)} %bitcast.13, s32[4,512]{1,0:T(4,128)S(1)} %copy-done.5, f32[3,128]{1,0:T(4,128)S(1)} %copy-done.9, bf16[128,512]{1,0:T(8,128)(2,1)S(1)} %copy-done.2), custom_call_target="tpu_custom_call" | custom-call | tf_op jit(solution)/shard_map/pallas_call | solution.py:109
  5.9 30.6 %all_to_all.21 = bf16[128,2,2048]{2,1,0:T(2,128)(2,1)S(1)} all-to-all(bf16[128,2,2048]{2,1,0:T(2,128)(2,1)S(1)} %shard_map.91), channel_id=1, replica_groups=mesh['dap'=128] {'dap'}, dimensions={0} | all-to-all | bytes 2097152 | tf_op jit(solution)/shard_map/all_to_all | solution.py:97
  36.6 4.1 %slice_reduce_fusion = (bf16[128,2048]{1,0:T(8,128)(2,1)S(1)}, bf16[128,1,2048]{2,1,0:T(2,128)(2,1)S(1)}) fusion(bf16[128,2,2048]{2,1,0:T(2,128)(2,1)S(1)} %all_to_all.21), kind=kLoop, calls=%fused_computation | loop fusion | bytes 2097152 | tf_op jit(solution)/shard_map/slice | solution.py:119
  40.7 0.3 reshape_squeeze.3.right_ref
  41.0 0.3 copy.24
  41.3 0.0 copy-start.11
  41.3 0.8 shard_map.92
  42.2 0.5 broadcast.1
  42.7 1.0 reduce.2
  43.7 1.2 reshape.17
  44.9 4.4 %all-to-all-start.1 = ((bf16[128,2,1024]{2,1,0:T(2,128)(2,1)}), bf16[128,2,1024]{2,1,0:T(2,128)(2,1)S(1)}, u32[]{:S(2)}, u32[]{:S(2)}) async-start(bf16[128,2,1024]{2,1,0:T(2,128)(2,1)} %reshape.17), calls=%async_computation.1 | async-start | bytes 1048576 | tf_op jit(solution)/shard_map/all_to_all | solution.py:97
  49.3 0.0 copy-done.11
  49.3 0.1 copy.18.wb_ref
  49.4 13.7 %all-to-all-done.1 = bf16[128,2,1024]{2,1,0:T(2,128)(2,1)S(1)} async-done(((bf16[128,2,1024]{2,1,0:T(2,128)(2,1)}), bf16[128,2,1024]{2,1,0:T(2,128)(2,1)S(1)}, u32[]{:S(2)}, u32[]{:S(2)}) %all-to-all-start.1) | async-done | bytes 524320 | tf_op jit(solution)/shard_map/all_to_all | solution.py:97
  63.2 0.4 reshape.18
  63.6 0.3 copy.25
  63.9 0.0 copy-done.1
  63.9 0.0 copy-done.7
  63.9 0.0 copy-done.8
  63.9 0.0 copy-done.10
  63.9 3.7 %shard_map.93 = (bf16[2048,128]{1,0:T(8,128)(2,1)S(1)}, bf16[2048,128]{1,0:T(8,128)(2,1)S(1)}, bf16[4,2048]{1,0:T(4,128)(2,1)S(1)}) custom-call(bf16[128,2048]{1,0:T(8,128)(2,1)S(1)} %bitcast.11, bf16[2048,128]{1,0:T(8,128)(2,1)S(1)} %bitcast.14, f32[3,128]{1,0:T(4,128)S(1)} %copy-done.10, bf16[128,128]{1,0:T(8,128)(2,1)S(1)} %copy-done.7, ...), custom_call_target="tpu_custom_call" | custom-call | tf_op jit(solution)/shard_map/pallas_call | solution.py:126
  67.7 1.0 broadcast_in_dim.8
  68.8 34.8 %all_to_all.22 = bf16[128,4,4,512]{3,2,1,0:T(4,128)(2,1)S(1)} all-to-all(bf16[128,4,4,512]{3,2,1,0:T(4,128)(2,1)S(1)} %broadcast_in_dim.8), channel_id=1, replica_groups=mesh['dap'=128] {'dap'}, dimensions={0} | all-to-all | bytes 4194304 | tf_op jit(solution)/shard_map/all_to_all | solution.py:97
  103.6 2.1 %copy.19 = bf16[4,128,4,512]{3,2,1,0:T(4,128)(2,1)} copy(bf16[4,128,4,512]{3,2,0,1:T(4,128)(2,1)S(1)} %bitcast.15) | data formatting | bytes 4194304 | tf_op jit(solution)/shard_map/transpose | solution.py:146
  105.7 2.6 %reshape.14.bias_ref = bf16[4,512,512]{2,1,0:T(8,128)(2,1)S(1)} reshape(bf16[4,128,4,512]{3,2,1,0:T(4,128)(2,1)} %copy.19) | data formatting | bytes 4194304 | tf_op jit(solution)/shard_map/reshape | solution.py:146
  108.2 0.0 copy-done.3
  108.2 0.0 copy-done.4
  108.3 9.8 %shard_map.94 = bf16[2048,128]{1,0:T(8,128)(2,1)} custom-call(bf16[2048,128]{1,0:T(8,128)(2,1)S(1)} %get-tuple-element.8.normed_ref, bf16[2048,128]{1,0:T(8,128)(2,1)S(1)} %get-tuple-element.9.mid_ref, s32[4,512]{1,0:T(4,128)S(1)} %copy-done.6, bf16[4,512,512]{2,1,0:T(8,128)(2,1)S(1)} %reshape.14.bias_ref, bf16[128,512]{1,0:T(8,128)(2,1)S(1)} %copy-done.3, ...), custom_call_target="tpu_custom_call" | custom-call | tf_op jit(solution)/shard_map/pallas_call | solution.py:147
  (13 shorter events, 0.0 us)
Async XLA Ops:
  0.0 1.0 copy-start
  1.0 0.9 copy-start.2
  1.9 0.7 copy-start.5
  2.6 0.7 copy-start.9
  41.3 8.0 %copy-start.11 = (bf16[128,4]{0,1:T(4,128)(2,1)S(1)}, bf16[128,4]{0,1:T(4,128)(2,1)}, u32[]{:S(2)}) copy-start(bf16[128,4]{0,1:T(4,128)(2,1)} %param.16) | copy-start | bytes 3076
  44.8 19.1 %copy-start.1 = (bf16[4,512,128]{2,1,0:T(8,128)(2,1)S(1)}, bf16[4,512,128]{2,1,0:T(8,128)(2,1)}, u32[]{:S(2)}) copy-start(bf16[4,512,128]{2,1,0:T(8,128)(2,1)} %param.9) | copy-start | bytes 1572868
  44.8 19.1 %copy-start.7 = (bf16[128,128]{1,0:T(8,128)(2,1)S(1)}, bf16[128,128]{1,0:T(8,128)(2,1)}, u32[]{:S(2)}) copy-start(bf16[128,128]{1,0:T(8,128)(2,1)} %wg_ref.1) | copy-start | bytes 98308
  44.8 19.1 %copy-start.8 = (bf16[128,128]{1,0:T(8,128)(2,1)S(1)}, bf16[128,128]{1,0:T(8,128)(2,1)}, u32[]{:S(2)}) copy-start(bf16[128,128]{1,0:T(8,128)(2,1)} %wo_ref.1) | copy-start | bytes 98308
  44.8 19.1 %copy-start.10 = (f32[3,128]{1,0:T(4,128)S(1)}, f32[3,128]{1,0:T(4,128)}, u32[]{:S(2)}) copy-start(f32[3,128]{1,0:T(4,128)} %gains_ref.3) | copy-start | bytes 4612
  44.9 18.3 %all-to-all-start.1 = ((bf16[128,2,1024]{2,1,0:T(2,128)(2,1)}), bf16[128,2,1024]{2,1,0:T(2,128)(2,1)S(1)}, u32[]{:S(2)}, u32[]{:S(2)}) async-start(bf16[128,2,1024]{2,1,0:T(2,128)(2,1)} %reshape.17), calls=%async_computation.1 | async-start | bytes 1048576 | tf_op jit(solution)/shard_map/all_to_all | solution.py:97
  105.6 2.6 %copy-start.3 = (bf16[128,512]{1,0:T(8,128)(2,1)S(1)}, bf16[128,512]{1,0:T(8,128)(2,1)}, u32[]{:S(2)}) copy-start(bf16[128,512]{1,0:T(8,128)(2,1)} %win_ref.1) | copy-start | bytes 393220
  105.6 2.6 %copy-start.4 = (bf16[128,128]{1,0:T(8,128)(2,1)S(1)}, bf16[128,128]{1,0:T(8,128)(2,1)}, u32[]{:S(2)}) copy-start(bf16[128,128]{1,0:T(8,128)(2,1)} %wout_ref.1) | copy-start | bytes 98308
  105.6 2.6 %copy-start.6 = (s32[4,512]{1,0:T(4,128)S(1)}, s32[4,512]{1,0:T(4,128)}, u32[]{:S(2)}) copy-start(s32[4,512]{1,0:T(4,128)} %mask_ref.3) | copy-start | bytes 24580

commit v2 on v0

v2 whole, which is shorter than its diff:
```python
import functools
import math

import jax
import jax.numpy as jnp
from jax import lax
from jax.experimental import pallas as pl
from jax.experimental.pallas import tpu as pltpu
from jax.sharding import PartitionSpec as P

F32 = jnp.float32
BF16 = jnp.bfloat16
VMEM_LIMIT = 40 * 1024 * 1024
LOG2E = math.log2(math.e)
TILE = 8


def dot(a, b, ca, cb):
    return lax.dot_general(a, b, (((ca,), (cb,)), ((), ())), preferred_element_type=F32)


def sigmoid(x):
    return 0.5 + 0.5 * jnp.tanh(0.5 * x)


def norm_rows(values, gain):
    mean = jnp.mean(values, axis=-1, keepdims=True)
    centered = values - mean
    var = jnp.mean(centered * centered, axis=-1, keepdims=True)
    return centered * lax.rsqrt(var + 1e-05) * gain


def put_rows(scratch, start, stride, values):
    for lane in range(values.shape[1] // 128):
        scratch[lane, pl.ds(start, values.shape[0], stride=stride), :] = values[:, lane * 128 : (lane + 1) * 128]


def get_rows(scratch, start, size, stride):
    return jnp.concatenate(
        [scratch[lane, pl.ds(start, size, stride=stride), :] for lane in range(scratch.shape[0])], axis=1
    )


def spill(scratch, values):
    for lane in range(scratch.shape[0]):
        part = values[:, :, lane * 128 : (lane + 1) * 128].astype(F32)
        scratch[lane] = part.reshape(scratch.shape[1], 128)


def fill(out_ref, scratch):
    for lane in range(scratch.shape[0]):
        part = scratch[lane].reshape(out_ref.shape[0], TILE, 128)
        out_ref[:, :, lane * 128 : (lane + 1) * 128] = part.astype(BF16)


def edges_kernel(pair_ref, mask_ref, gains_ref, w_ref, out_ref, scratch):
    rows, total = mask_ref.shape
    hidden = out_ref.shape[0]
    for row in range(rows):
        pair = pair_ref[row].astype(F32)
        normed = norm_rows(pair, gains_ref[0:1, :]).astype(BF16)
        edges = dot(w_ref[...], normed, 0, 1)
        mask = mask_ref[row : row + 1, :].astype(F32)
        for side in range(2):
            gate = edges[2 * side * hidden : (2 * side + 1) * hidden]
            value = edges[(2 * side + 1) * hidden : (2 * side + 2) * hidden]
            put_rows(scratch, side * rows + row, TILE, mask * sigmoid(gate) * value)
    fill(out_ref, scratch)


def product_kernel(sides_ref, out_ref, scratch, right_ref, prod_ref):
    devices, _, total = sides_ref.shape
    rows = total // devices
    half = total // 2
    spill(scratch, sides_ref[...])
    for row in range(rows):
        put_rows(right_ref, row, rows, get_rows(scratch, rows + row, devices, TILE))
    right = jnp.concatenate([right_ref[lane] for lane in range(total // 128)], axis=1).astype(BF16)
    for row in range(rows):
        left = get_rows(scratch, row, devices, TILE).astype(BF16)
        product = dot(left, right, 1, 1)
        for part in range(2):
            put_rows(prod_ref, 2 * row + part, TILE, product[:, part * half : (part + 1) * half])
    fill(out_ref, prod_ref)


def middle_kernel(
    prod_ref, pair_ref, gains_ref, wg_ref, wo_ref, wb_ref, mid_ref, normed_ref, bias_ref, scratch, bias_f
):
    rows, total, width = pair_ref.shape
    heads = wb_ref.shape[1]
    devices = bias_ref.shape[0]
    spill(scratch, prod_ref[...])
    gain = gains_ref[1:2, :].T
    for row in range(rows):
        prod = jnp.concatenate(
            [get_rows(scratch, 2 * row + part, width, TILE) for part in range(2)], axis=1
        )
        mean = jnp.mean(prod, axis=0, keepdims=True)
        centered = prod - mean
        var = jnp.mean(centered * centered, axis=0, keepdims=True)
        prod_normed = (centered * lax.rsqrt(var + 1e-05) * gain).astype(BF16)
        pair = pair_ref[row].astype(F32)
        normed = norm_rows(pair, gains_ref[0:1, :]).astype(BF16)
        gate = sigmoid(dot(normed, wg_ref[...], 1, 0))
        mid = (pair + gate * dot(prod_normed, wo_ref[...], 0, 0)).astype(BF16)
        mid_ref[row] = mid
        mid_normed = norm_rows(mid.astype(F32), gains_ref[2:3, :]).astype(BF16)
        normed_ref[row] = mid_normed
        bias = dot(wb_ref[...], mid_normed, 0, 1)
        for head in range(heads):
            bias_f[head * rows + row : head * rows + row + 1, :] = bias[head : head + 1, :]
    for part in range(2):
        block = bias_f[part * TILE : (part + 1) * TILE, :].astype(BF16)
        for pair_of in range(devices // 2):
            bias_ref[2 * pair_of + part] = block


def attention_kernel(
    head_dim, last, first_head, normed_ref, mask_ref, bias_ref, win_ref, *rest
):
    if last:
        mid_ref, part_ref, wout_ref, out_ref, scratch, bias_f = rest
    else:
        out_ref, scratch, bias_f = rest
    rows, total, width = normed_ref.shape
    devices = bias_ref.shape[0]
    own = TILE // rows
    spill(scratch, bias_ref[...])
    for head in range(own):
        for row in range(rows):
            values = get_rows(scratch, head * rows + row, devices, TILE) * LOG2E
            put_rows(bias_f.at[head], row, rows, values)
    base = first_head[0]
    lane_head = lax.broadcasted_iota(jnp.int32, (1, width), 1) // head_dim
    scale = LOG2E / math.sqrt(head_dim)
    for row in range(rows):
        packed = dot(normed_ref[row], win_ref[...], 1, 0)
        query = (packed[:, 0:width] * scale).astype(BF16)
        key = packed[:, width : 2 * width].astype(BF16)
        value = packed[:, 2 * width : 3 * width].astype(BF16)
        mask = (1000000000.0 * LOG2E) * (mask_ref[row : row + 1, :].astype(F32) - 1.0)
        mixed = jnp.zeros((total, 2 * width), F32)
        for head in range(own):
            pick = (lane_head == base + head).astype(BF16)
            bias = jnp.concatenate([bias_f[head, lane] for lane in range(total // 128)], axis=1)
            logits = dot(query * pick, key, 1, 1) + bias + mask
            top = jnp.max(logits, axis=-1, keepdims=True)
            expo = jnp.exp2(logits - top).astype(BF16)
            both = jnp.concatenate([value * pick, jnp.broadcast_to(pick, value.shape)], axis=1)
            mixed = mixed + dot(expo, both, 1, 0)
        mine = (lane_head >= base) & (lane_head < base + own)
        share = jnp.where(mine, mixed[:, :width] / mixed[:, width:], 0.0)
        if last:
            att_gate = sigmoid(packed[:, 3 * width : 4 * width])
            attended = (att_gate * (share + part_ref[row])).astype(BF16)
            update = dot(attended, wout_ref[...], 1, 0)
            out_ref[row] = (mid_ref[row].astype(F32) + update).astype(BF16)
        else:
            out_ref[row] = share


def params():
    return pltpu.CompilerParams(vmem_limit_bytes=VMEM_LIMIT)


def call(kernel, out_shape, scratch, n_args, scalar_at=None):
    specs = [
        pl.BlockSpec(memory_space=pltpu.SMEM if at == scalar_at else pltpu.VMEM) for at in range(n_args)
    ]
    return pl.pallas_call(
        kernel,
        in_specs=specs,
        out_specs=jax.tree.map(lambda _: pl.BlockSpec(memory_space=pltpu.VMEM), out_shape),
        out_shape=out_shape,
        scratch_shapes=scratch,
        compiler_params=params(),
    )


def exchange(array):
    return lax.all_to_all(array, "dap", 0, 0, tiled=True)


def per_device(
    pair, pair_mask, norm_gains, w_edges, w_tri_gate, w_tri_out, w_attn_in, w_tri_bias, w_attn_out
):
    rows, total, width = pair.shape
    hidden = w_tri_out.shape[0]
    heads = w_tri_bias.shape[1]
    devices = total // rows
    lanes = total // 128
    shape = jax.ShapeDtypeStruct
    tall = pltpu.VMEM((lanes, devices * TILE, 128), F32)
    square = pltpu.VMEM((lanes, total, 128), F32)
    short = pltpu.VMEM((lanes // 2, devices * TILE, 128), F32)
    sides = call(edges_kernel, shape((hidden, TILE, total), BF16), [tall], 4)(
        pair, pair_mask, norm_gains, w_edges
    )
    sides = exchange(sides)
    product = call(
        product_kernel, shape((devices, TILE, total // 2), BF16), [tall, square, short], 1
    )(sides)
    product = exchange(product)
    mid, mid_normed, bias = call(
        middle_kernel,
        [
            shape((rows, total, width), BF16),
            shape((rows, total, width), BF16),
            shape((devices, TILE, total), BF16),
        ],
        [short, pltpu.VMEM((2 * TILE, total), F32)],
        6,
    )(product, pair, norm_gains, w_tri_gate, w_tri_out, w_tri_bias)
    mine = exchange(bias)
    swap = [(d, d ^ 1) for d in range(devices)]
    other = lax.ppermute(mine, "dap", swap)
    own = heads // 2
    core = lax.rem(lax.axis_index("dap"), 2)
    scratch = [tall, pltpu.VMEM((own, lanes, total, 128), F32)]
    part = call(
        functools.partial(attention_kernel, width // heads, False),
        shape((rows, total, width), F32),
        scratch,
        5,
        0,
    )(jnp.reshape(core * own, (1,)), mid_normed, pair_mask, mine, w_attn_in)
    return call(
        functools.partial(attention_kernel, width // heads, True),
        shape((rows, total, width), BF16),
        scratch,
        8,
        0,
    )(
        jnp.reshape((1 - core) * own, (1,)),
        mid_normed,
        pair_mask,
        other,
        w_attn_in,
        mid,
        part,
        w_attn_out,
    )


def solution(mesh):
    placed = (P("dap", None, None), P("dap", None), P(), P(), P(), P(), P(), P(), P())
    return jax.shard_map(
        per_device, mesh=mesh, in_specs=placed, out_specs=P("dap", None, None), check_vma=False
    )
```

time: 428 us -> 95.5 us (0.22)
  waiting for transfers between devices: 233 us -> 13.7 us
  local copies, waits for them, and re-layouts: 105 us -> 4.18 us
  matrix products: 63.4 us -> 0 us
  blocking collectives: 0 us -> 54.3 us
  Pallas kernels: 0 us -> 17.5 us
  between operations: 13.6 us -> 0.1 us
  other arithmetic: 9.01 us -> 0 us
  starting transfers between devices: 0.04 us -> 5.3 us
    all_gather x2 -> x0, waiting for transfers between devices: 233 us -> none  [the longest x1 168 us: per_device(): gathered = lax.all_gather(right, 'dap', axis=0, tiled=True)]
    all_gather x1 -> x0, local copies, waits for them, and re-layouts: 88.9 us -> none  [per_device(): gathered = lax.all_gather(right, 'dap', axis=0, tiled=True)]
    dot_general x21 -> x0, matrix products: 63.4 us -> none  [the longest x1 25.5 us: per_device(): jnp.einsum('ikc,jkc->ijc', left, gathered, preferred_element_type=jnp.flo...]
    all_to_all x0 -> x2, blocking collectives: none -> 54.3 us  [exchange(): return lax.all_to_all(array, 'dap', 0, 0, tiled=True)]
    pallas_call x0 -> x5, Pallas kernels: none -> 17.5 us  [the longest x1 6.76 us: per_device(): call(functools.partial(attention_kernel, width // heads, True), shape((ro...]
    all_to_all x0 -> x1, waiting for transfers between devices: none -> 13.7 us  [exchange(): return lax.all_to_all(array, 'dap', 0, 0, tiled=True)]
    while x9 -> x0, local copies, waits for them, and re-layouts: 12.7 us -> none
    all_to_all x0 -> x1, starting transfers between devices: none -> 4.43 us  [exchange(): return lax.all_to_all(array, 'dap', 0, 0, tiled=True)]
  transfers between devices with their start and end apart: 2 -> 2, of which waited for: 2 -> 1; matrix products, arithmetic and copies ran while one was open for 0% -> 0% of each run, Pallas kernels for 0% -> 4%
where the time goes in v2:
time: 95.5 us; the launch traced here: 95.1 us
  blocking collectives  54.3 us (57%)
  Pallas kernels  17.5 us (18%)
  waiting for transfers between devices  13.7 us (14%)
  starting transfers between devices  5.3 us (6%)
  local copies, waits for them, and re-layouts  4.18 us (4%)
    all_to_all x2, blocking collectives, exchange(): return lax.all_to_all(array, 'dap', 0, 0, tiled=True)  54.3 us
    all_to_all x1, waiting for transfers between devices, exchange(): return lax.all_to_all(array, 'dap', 0, 0, tiled=True)  13.7 us
    pallas_call x1, Pallas kernels, per_device(): call(functools.partial(attention_kernel, width // heads, True), shape((ro...  6.76 us
    all_to_all x1, starting transfers between devices, exchange(): return lax.all_to_all(array, 'dap', 0, 0, tiled=True)  4.43 us
    unnamed x25, local copies, waits for them, and re-layouts  4.18 us
    pallas_call x1, Pallas kernels, per_device(): call(functools.partial(attention_kernel, width // heads, False), shape((r...  4.07 us
    pallas_call x1, Pallas kernels, per_device(): call(middle_kernel, [shape((rows, total, width), BF16), shape((rows, tota...  2.89 us
    pallas_call x1, Pallas kernels, per_device(): call(product_kernel, shape((devices, TILE, total // 2), BF16), [tall, squ...  1.98 us
  transfers between devices with their start and end apart: 2, of which 1 were waited for; matrix products, arithmetic and copies ran while one was open for 0% of the time, Pallas kernels for 4%

profile of v2, /device:TPU:1, one launch (start us, length us, event | category | flops | bytes accessed | tf_op | source)
XLA Modules:
  0.0 95.1 jit_solution(3747326124747780510)
XLA Ops:
  0.0 0.0 copy-start
  0.0 1.0 %copy-done = bf16[4,512,128]{2,1,0:T(8,128)(2,1)S(1)} copy-done((bf16[4,512,128]{2,1,0:T(8,128)(2,1)S(1)}, bf16[4,512,128]{2,1,0:T(8,128)(2,1)}, u32[]{:S(2)}) %copy-start) | copy-done | bytes 524312
  1.0 0.0 copy-start.3
  1.0 0.9 copy-done.3
  1.9 0.0 copy-start.4
  1.9 0.7 copy-done.4
  2.6 0.7 copy-done.9
  3.3 1.8 %shard_map.91 = bf16[128,8,512]{2,1,0:T(8,128)(2,1)S(1)} custom-call(bf16[4,512,128]{2,1,0:T(8,128)(2,1)S(1)} %copy-done, s32[4,512]{1,0:T(4,128)S(1)} %copy-done.4, f32[3,128]{1,0:T(4,128)S(1)} %copy-done.9, bf16[128,512]{1,0:T(8,128)(2,1)S(1)} %copy-done.3), custom_call_target="tpu_custom_call" | custom-call | tf_op jit(solution)/shard_map/pallas_call | solution.py:197
  5.2 30.6 %all_to_all.15.sides_ref = bf16[128,8,512]{2,1,0:T(8,128)(2,1)S(1)} all-to-all(bf16[128,8,512]{2,1,0:T(8,128)(2,1)S(1)} %shard_map.91), channel_id=1, replica_groups=mesh['dap'=128] {'dap'}, dimensions={0} | all-to-all | bytes 2097152 | tf_op jit(solution)/shard_map/all_to_all | solution.py:182
  35.8 2.0 %shard_map.92 = bf16[128,8,256]{2,1,0:T(8,128)(2,1)} custom-call(bf16[128,8,512]{2,1,0:T(8,128)(2,1)S(1)} %all_to_all.15.sides_ref), custom_call_target="tpu_custom_call" | custom-call | tf_op jit(solution)/shard_map/pallas_call | solution.py:201
  37.8 0.0 copy-start.11
  37.8 0.0 copy-start.1
  37.8 0.0 copy-start.8
  37.8 4.4 %all-to-all-start.1 = ((bf16[128,8,256]{2,1,0:T(8,128)(2,1)}), bf16[128,8,256]{2,1,0:T(8,128)(2,1)S(1)}, u32[]{:S(2)}, u32[]{:S(2)}) async-start(bf16[128,8,256]{2,1,0:T(8,128)(2,1)} %shard_map.92), calls=%async_computation.1 | async-start | bytes 1048576 | tf_op jit(solution)/shard_map/all_to_all | solution.py:182
  42.2 0.0 copy-done.11
  42.3 0.0 copy-start.7
  42.3 0.1 copy.10.wb_ref
  42.4 13.7 %all-to-all-done.1.prod_ref = bf16[128,8,256]{2,1,0:T(8,128)(2,1)S(1)} async-done(((bf16[128,8,256]{2,1,0:T(8,128)(2,1)}), bf16[128,8,256]{2,1,0:T(8,128)(2,1)S(1)}, u32[]{:S(2)}, u32[]{:S(2)}) %all-to-all-start.1) | async-done | bytes 524320 | tf_op jit(solution)/shard_map/all_to_all | solution.py:182
  56.1 0.0 copy-done.1
  56.1 0.0 copy-done.8
  56.1 0.0 copy-done.10
  56.1 0.0 copy-done.7
  56.1 2.9 %shard_map.93 = (bf16[4,512,128]{2,1,0:T(8,128)(2,1)S(1)}, bf16[4,512,128]{2,1,0:T(8,128)(2,1)S(1)}, bf16[128,8,512]{2,1,0:T(8,128)(2,1)S(1)}) custom-call(bf16[128,8,256]{2,1,0:T(8,128)(2,1)S(1)} %all-to-all-done.1.prod_ref, bf16[4,512,128]{2,1,0:T(8,128)(2,1)S(1)} %copy-done.1, f32[3,128]{1,0:T(4,128)S(1)} %copy-done.10, bf16[128,128]{1,0:T(8,128)(2,1)S(1)} %copy-done.7, ...), custom_call_target="tpu_custom_call" | custom-call | tf_op jit(solution)/shard_map/pallas_call | solution.py:205
  59.0 0.0 copy-start.2
  59.0 23.7 %all_to_all.16.bias_ref = bf16[128,8,512]{2,1,0:T(8,128)(2,1)S(1)} all-to-all(bf16[128,8,512]{2,1,0:T(8,128)(2,1)S(1)} %get-tuple-element.9), channel_id=1, replica_groups=mesh['dap'=128] {'dap'}, dimensions={0} | all-to-all | bytes 2097152 | tf_op jit(solution)/shard_map/all_to_all | solution.py:182
  82.7 0.9 collective-permute-start
  83.6 0.0 copy-done.2
  83.6 0.7 copy-done.5
  84.3 4.1 %shard_map.94.rest_1_ = f32[4,512,128]{2,1,0:T(8,128)S(1)} custom-call(s32[1]{0:T(128)} %bitcast.1.first_head, bf16[4,512,128]{2,1,0:T(8,128)(2,1)S(1)} %get-tuple-element.8.normed_ref, s32[4,512]{1,0:T(4,128)S(1)} %copy-done.5, bf16[128,8,512]{2,1,0:T(8,128)(2,1)S(1)} %all_to_all.16.bias_ref, bf16[128,512]{1,0:T(8,128)(2,1)S(1)} %copy-done.2), custom_call_target="tpu_custom_call" | custom-call | tf_op jit(solution)/shard_map/pallas_call | solution.py:221
  88.4 0.0 collective-permute-done.bias_ref
  88.4 0.0 copy-done.6
  88.4 6.8 %shard_map.95 = bf16[4,512,128]{2,1,0:T(8,128)(2,1)} custom-call(s32[1]{0:T(128)} %bitcast.first_head, bf16[4,512,128]{2,1,0:T(8,128)(2,1)S(1)} %get-tuple-element.8.normed_ref, s32[4,512]{1,0:T(4,128)S(1)} %copy-done.5, bf16[128,8,512]{2,1,0:T(8,128)(2,1)S(1)} %collective-permute-done.bias_ref, bf16[128,512]{1,0:T(8,128)(2,1)S(1)} %copy-done.2, ...), custom_call_target="tpu_custom_call" | custom-call | tf_op jit(solution)/shard_map/pallas_call | solution.py:228
  (4 shorter events, 0.0 us)
Async XLA Ops:
  0.0 1.0 %copy-start = (bf16[4,512,128]{2,1,0:T(8,128)(2,1)S(1)}, bf16[4,512,128]{2,1,0:T(8,128)(2,1)}, u32[]{:S(2)}) copy-start(bf16[4,512,128]{2,1,0:T(8,128)(2,1)} %pair_ref.3) | copy-start | bytes 1572868
  1.0 0.9 copy-start.3
  1.9 0.7 copy-start.4
  2.6 0.7 copy-start.9
  37.8 4.5 %copy-start.11 = (bf16[128,4]{0,1:T(4,128)(2,1)S(1)}, bf16[128,4]{0,1:T(4,128)(2,1)}, u32[]{:S(2)}) copy-start(bf16[128,4]{0,1:T(4,128)(2,1)} %param.16) | copy-start | bytes 3076
  37.8 18.3 %copy-start.1 = (bf16[4,512,128]{2,1,0:T(8,128)(2,1)S(1)}, bf16[4,512,128]{2,1,0:T(8,128)(2,1)}, u32[]{:S(2)}) copy-start(bf16[4,512,128]{2,1,0:T(8,128)(2,1)} %pair_ref.3) | copy-start | bytes 1572868
  37.8 18.3 %copy-start.8 = (bf16[128,128]{1,0:T(8,128)(2,1)S(1)}, bf16[128,128]{1,0:T(8,128)(2,1)}, u32[]{:S(2)}) copy-start(bf16[128,128]{1,0:T(8,128)(2,1)} %wo_ref.1) | copy-start | bytes 98308
  37.8 18.3 %copy-start.10 = (f32[3,128]{1,0:T(4,128)S(1)}, f32[3,128]{1,0:T(4,128)}, u32[]{:S(2)}) copy-start(f32[3,128]{1,0:T(4,128)} %gains_ref.3) | copy-start | bytes 4612
  37.8 18.3 %all-to-all-start.1 = ((bf16[128,8,256]{2,1,0:T(8,128)(2,1)}), bf16[128,8,256]{2,1,0:T(8,128)(2,1)S(1)}, u32[]{:S(2)}, u32[]{:S(2)}) async-start(bf16[128,8,256]{2,1,0:T(8,128)(2,1)} %shard_map.92), calls=%async_computation.1 | async-start | bytes 1048576 | tf_op jit(solution)/shard_map/all_to_all | solution.py:182
  42.3 13.9 %copy-start.7 = (bf16[128,128]{1,0:T(8,128)(2,1)S(1)}, bf16[128,128]{1,0:T(8,128)(2,1)}, u32[]{:S(2)}) copy-start(bf16[128,128]{1,0:T(8,128)(2,1)} %wg_ref.1) | copy-start | bytes 98308
  59.0 24.6 %copy-start.2 = (bf16[128,512]{1,0:T(8,128)(2,1)S(1)}, bf16[128,512]{1,0:T(8,128)(2,1)}, u32[]{:S(2)}) copy-start(bf16[128,512]{1,0:T(8,128)(2,1)} %win_ref.3) | copy-start | bytes 393220
  82.7 5.7 %collective-permute-start = (bf16[128,8,512]{2,1,0:T(8,128)(2,1)S(1)}, bf16[128,8,512]{2,1,0:T(8,128)(2,1)S(1)}, u32[]{:S(2)}, u32[]{:S(2)}) collective-permute-start(bf16[128,8,512]{2,1,0:T(8,128)(2,1)S(1)} %all_to_all.16.bias_ref), channel_id=1, source_target_pairs={{0,1},{1,0},{2,3},{3,2},{4,5},{5,4},{6,7},{7,6},{8,9},{9,8},{10,11... | collective-permute-start | bytes 3145736 | tf_op jit(solution)/shard_map/ppermute | solution.py:217
  83.6 0.7 copy-start.5
  84.3 4.1 %copy-start.6 = (bf16[128,128]{1,0:T(8,128)(2,1)S(1)}, bf16[128,128]{1,0:T(8,128)(2,1)}, u32[]{:S(2)}) copy-start(bf16[128,128]{1,0:T(8,128)(2,1)} %rest_2_.1) | copy-start | bytes 98308

commit v3 on v2

v3 whole, which is shorter than its diff:
```python
import functools
import math

import jax
import jax.numpy as jnp
from jax import lax
from jax.experimental import pallas as pl
from jax.experimental.pallas import tpu as pltpu
from jax.sharding import PartitionSpec as P

F32 = jnp.float32
BF16 = jnp.bfloat16
VMEM_LIMIT = 40 * 1024 * 1024
EDGES_LIMIT = 60 * 1024 * 1024
LOG2E = math.log2(math.e)
TILE = 8


def dot(a, b, ca, cb):
    return lax.dot_general(a, b, (((ca,), (cb,)), ((), ())), preferred_element_type=F32)


def sigmoid(x):
    return 0.5 + 0.5 * jnp.tanh(0.5 * x)


def norm_rows(values, gain):
    mean = jnp.mean(values, axis=-1, keepdims=True)
    centered = values - mean
    var = jnp.mean(centered * centered, axis=-1, keepdims=True)
    return centered * lax.rsqrt(var + 1e-05) * gain


def put_rows(scratch, start, stride, values):
    for lane in range(values.shape[1] // 128):
        scratch[lane, pl.ds(start, values.shape[0], stride=stride), :] = values[:, lane * 128 : (lane + 1) * 128]


def get_rows(scratch, start, size, stride):
    return jnp.concatenate(
        [scratch[lane, pl.ds(start, size, stride=stride), :] for lane in range(scratch.shape[0])], axis=1
    )


def spill(scratch, values):
    for lane in range(scratch.shape[0]):
        part = values[:, :, lane * 128 : (lane + 1) * 128].astype(F32)
        scratch[lane] = part.reshape(scratch.shape[1], 128)


def fill(out_ref, scratch):
    for lane in range(scratch.shape[0]):
        part = scratch[lane].reshape(out_ref.shape[0], TILE, 128)
        out_ref[:, :, lane * 128 : (lane + 1) * 128] = part.astype(BF16)


def edges_kernel(pair_ref, mask_ref, gains_ref, w_ref, out_ref, scratch):
    rows, total = mask_ref.shape
    hidden = out_ref.shape[0]
    normed = [norm_rows(pair_ref[row].astype(F32), gains_ref[0:1, :]).astype(BF16) for row in range(rows)]
    edges = [dot(w_ref[...], normed[row], 0, 1) for row in range(rows)]
    for row in range(rows):
        mask = mask_ref[row : row + 1, :].astype(F32)
        for side in range(2):
            gate = edges[row][2 * side * hidden : (2 * side + 1) * hidden]
            value = edges[row][(2 * side + 1) * hidden : (2 * side + 2) * hidden]
            put_rows(scratch, side * rows + row, TILE, mask * sigmoid(gate) * value)
    fill(out_ref, scratch)


def product_kernel(sides_ref, out_ref, scratch, right_ref, prod_ref):
    devices, _, total = sides_ref.shape
    rows = total // devices
    half = total // 2
    spill(scratch, sides_ref[...])
    for row in range(rows):
        put_rows(right_ref, row, rows, get_rows(scratch, rows + row, devices, TILE))
    right = jnp.concatenate([right_ref[lane] for lane in range(total // 128)], axis=1).astype(BF16)
    left = [get_rows(scratch, row, devices, TILE).astype(BF16) for row in range(rows)]
    product = [dot(left[row], right, 1, 1) for row in range(rows)]
    for row in range(rows):
        for part in range(2):
            put_rows(prod_ref, 2 * row + part, TILE, product[row][:, part * half : (part + 1) * half])
    fill(out_ref, prod_ref)


def gate_kernel(pair_ref, gains_ref, wg_ref, out_ref):
    for row in range(pair_ref.shape[0]):
        normed = norm_rows(pair_ref[row].astype(F32), gains_ref[0:1, :]).astype(BF16)
        out_ref[row] = sigmoid(dot(normed, wg_ref[...], 1, 0))


def middle_kernel(
    prod_ref,
    pair_ref,
    gate_ref,
    gains_ref,
    mask_ref,
    wo_ref,
    wb_ref,
    mid_ref,
    normed_ref,
    masked_ref,
    bias_ref,
    scratch,
    bias_f,
):
    rows, total, width = pair_ref.shape
    heads = wb_ref.shape[0]
    devices = bias_ref.shape[0]
    spill(scratch, prod_ref[...])
    gain = gains_ref[1:2, :].T
    masked_ref[...] = (1000000000.0 * LOG2E) * (mask_ref[...].astype(F32) - 1.0)
    prod_normed = []
    for row in range(rows):
        prod = jnp.concatenate(
            [get_rows(scratch, 2 * row + part, width, TILE) for part in range(2)], axis=1
        )
        mean = jnp.mean(prod, axis=0, keepdims=True)
        centered = prod - mean
        var = jnp.mean(centered * centered, axis=0, keepdims=True)
        prod_normed.append((centered * lax.rsqrt(var + 1e-05) * gain).astype(BF16))
    update = [dot(prod_normed[row], wo_ref[...], 0, 0) for row in range(rows)]
    mid = [(pair_ref[row].astype(F32) + gate_ref[row] * update[row]).astype(BF16) for row in range(rows)]
    mid_normed = []
    for row in range(rows):
        mid_ref[row] = mid[row]
        mid_normed.append(norm_rows(mid[row].astype(F32), gains_ref[2:3, :]).astype(BF16))
        normed_ref[row] = mid_normed[row]
    bias = [dot(wb_ref[...], mid_normed[row], 1, 1) for row in range(rows)]
    for row in range(rows):
        for head in range(heads):
            bias_f[head * rows + row : head * rows + row + 1, :] = bias[row][head : head + 1, :]
    for part in range(2):
        block = bias_f[part * TILE : (part + 1) * TILE, :].astype(BF16)
        for pair_of in range(devices // 2):
            bias_ref[2 * pair_of + part] = block


def attend(head_dim, first_head, query_ref, key_ref, value_ref, gate_ref, bias_ref, masked_ref, scratch, bias_f):
    rows, total, width = value_ref.shape
    devices = bias_ref.shape[0]
    own = TILE // rows
    spill(scratch, bias_ref[...])
    for head in range(own):
        for row in range(rows):
            values = get_rows(scratch, head * rows + row, devices, TILE) * LOG2E
            put_rows(bias_f.at[head], row, rows, values)
    base = first_head[0]
    lane_head = lax.broadcasted_iota(jnp.int32, (1, width), 1) // head_dim
    mine = (lane_head >= base) & (lane_head < base + own)
    attended = []
    for row in range(rows):
        expos, boths = [], []
        for head in range(own):
            pick = (lane_head == base + head).astype(BF16)
            bias = jnp.concatenate([bias_f[head, lane] for lane in range(total // 128)], axis=1)
            logits = dot(query_ref[row] * pick, key_ref[row], 1, 1) + bias + masked_ref[row : row + 1, :]
            top = jnp.max(logits, axis=-1, keepdims=True)
            expos.append(jnp.exp2(logits - top).astype(BF16))
            value = value_ref[row]
            boths.append(
                jnp.concatenate([value * pick, jnp.broadcast_to(pick, value.shape)], axis=1)
            )
        mixed = dot(jnp.concatenate(expos, axis=1), jnp.concatenate(boths, axis=0), 1, 0)
        share = jnp.where(mine, mixed[:, :width] / mixed[:, width:], 0.0)
        attended.append((gate_ref[row] * share).astype(BF16))
    return attended


def own_heads_kernel(
    head_dim,
    first_head,
    normed_ref,
    bias_ref,
    masked_ref,
    win_ref,
    query_ref,
    key_ref,
    value_ref,
    gate_ref,
    out_ref,
    scratch,
    bias_f,
):
    rows, total, width = normed_ref.shape
    scale = LOG2E / math.sqrt(head_dim)
    packed = [dot(normed_ref[row], win_ref[...], 1, 0) for row in range(rows)]
    for row in range(rows):
        query_ref[row] = (packed[row][:, 0:width] * scale).astype(BF16)
        key_ref[row] = packed[row][:, width : 2 * width].astype(BF16)
        value_ref[row] = packed[row][:, 2 * width : 3 * width].astype(BF16)
        gate_ref[row] = sigmoid(packed[row][:, 3 * width : 4 * width])
    attended = attend(
        head_dim, first_head, query_ref, key_ref, value_ref, gate_ref, bias_ref, masked_ref, scratch, bias_f
    )
    for row in range(rows):
        out_ref[row] = attended[row]


def other_heads_kernel(
    head_dim,
    first_head,
    query_ref,
    key_ref,
    value_ref,
    gate_ref,
    bias_ref,
    masked_ref,
    mid_ref,
    part_ref,
    wout_ref,
    out_ref,
    scratch,
    bias_f,
    result,
    sems,
):
    rows = mid_ref.shape[0]
    attended = attend(
        head_dim, first_head, query_ref, key_ref, value_ref, gate_ref, bias_ref, masked_ref, scratch, bias_f
    )
    copies = []
    for row in range(rows):
        update = dot(attended[row] + part_ref[row], wout_ref[...], 1, 0)
        result[row] = (mid_ref[row].astype(F32) + update).astype(BF16)
        copies.append(pltpu.make_async_copy(result.at[row], out_ref.at[row], sems.at[row]))
        copies[row].start()
    for copy in copies:
        copy.wait()


def call(kernel, out_shape, scratch, n_args, scalars=0, limit=VMEM_LIMIT, out_space=pltpu.VMEM, cost=None):
    specs = [
        pl.BlockSpec(memory_space=pltpu.SMEM if at < scalars else pltpu.VMEM) for at in range(n_args)
    ]
    return pl.pallas_call(
        kernel,
        in_specs=specs,
        out_specs=jax.tree.map(lambda _: pl.BlockSpec(memory_space=out_space), out_shape),
        out_shape=out_shape,
        scratch_shapes=scratch,
        compiler_params=pltpu.CompilerParams(vmem_limit_bytes=limit),
        cost_estimate=cost,
    )


def cost(flops, bytes_accessed, transcendentals):
    return pl.CostEstimate(
        flops=flops, bytes_accessed=bytes_accessed, transcendentals=transcendentals
    )


def exchange(array):
    return lax.all_to_all(array, "dap", 0, 0, tiled=True)


def per_device(
    pair, pair_mask, norm_gains, w_edges, w_tri_gate, w_tri_out, w_attn_in, w_tri_bias, w_attn_out
):
    rows, total, width = pair.shape
    hidden = w_tri_out.shape[0]
    heads = w_tri_bias.shape[1]
    head_dim = width // heads
    own = heads // 2
    devices = total // rows
    lanes = total // 128
    shape = jax.ShapeDtypeStruct
    tall = pltpu.VMEM((lanes, devices * TILE, 128), F32)
    square = pltpu.VMEM((lanes, total, 128), F32)
    short = pltpu.VMEM((lanes // 2, devices * TILE, 128), F32)
    sides = call(
        edges_kernel, shape((hidden, TILE, total), BF16), [tall], 4, limit=EDGES_LIMIT
    )(pair, pair_mask, norm_gains, w_edges)
    sides = exchange(sides)
    product = call(
        product_kernel, shape((devices, TILE, total // 2), BF16), [tall, square, short], 1
    )(sides)
    product = exchange(product)
    gate = call(
        gate_kernel,
        shape((rows, total, width), F32),
        [],
        3,
        cost=cost(2 * rows * total * width * width, 4 << 20, rows * total * width),
    )(pair, norm_gains, w_tri_gate)
    like = shape((rows, total, width), BF16)
    wide = shape((rows, total, width), F32)
    mid, mid_normed, masked, bias = call(
        middle_kernel,
        [like, like, shape((rows, total), F32), shape((devices, TILE, total), BF16)],
        [short, pltpu.VMEM((2 * TILE, total), F32)],
        7,
    )(product, pair, gate, norm_gains, pair_mask, w_tri_out, w_tri_bias.T)
    mine = exchange(bias)
    swap = [(d, d ^ 1) for d in range(devices)]
    other = lax.ppermute(mine, "dap", swap)
    core = lax.rem(lax.axis_index("dap"), 2)
    mine_first = jnp.reshape(core * own, (1,))
    other_first = jnp.reshape((1 - core) * own, (1,))
    scratch = [tall, pltpu.VMEM((own, lanes, total, 128), F32)]
    query, key, value, att_gate, part = call(
        functools.partial(own_heads_kernel, head_dim),
        [like, like, like, wide, like],
        scratch,
        5,
        1,
    )(mine_first, mid_normed, mine, masked, w_attn_in)
    scratch = scratch + [pltpu.VMEM((rows, total, width), BF16), pltpu.SemaphoreType.DMA((rows,))]
    return call(
        functools.partial(other_heads_kernel, head_dim),
        like,
        scratch,
        10,
        1,
        out_space=pl.ANY,
    )(other_first, query, key, value, att_gate, other, masked, mid, part, w_attn_out)


def solution(mesh):
    placed = (P("dap", None, None), P("dap", None), P(), P(), P(), P(), P(), P(), P())
    return jax.shard_map(
        per_device, mesh=mesh, in_specs=placed, out_specs=P("dap", None, None), check_vma=False
    )
```

time: 95.5 us -> 89.5 us (0.937)
  local copies, waits for them, and re-layouts: 4.18 us -> 0.04 us
  Pallas kernels: 17.5 us -> 16.2 us
    unnamed x25 -> x16, local copies, waits for them, and re-layouts: 4.18 us -> 0.04 us
    pallas_call x4 -> x5, Pallas kernels: 15.6 us -> 14.2 us  [the longest x1 4.25 us: per_device(): call(functools.partial(other_heads_kernel, head_dim), like, scratch, 10,...]
  transfers between devices with their start and end apart: 2 -> 2, of which waited for: 1 -> 1; matrix products, arithmetic and copies ran while one was open for 0% -> 0% of each run, Pallas kernels for 4% -> 5%
where the time goes in v3:
time: 89.5 us; the launch traced here: 89.3 us
  blocking collectives  54.5 us (61%)
  Pallas kernels  16.2 us (18%)
  waiting for transfers between devices  13 us (15%)
  starting transfers between devices  5.29 us (6%)
    all_to_all x2, blocking collectives, exchange(): return lax.all_to_all(array, 'dap', 0, 0, tiled=True)  54.5 us
    all_to_all x1, waiting for transfers between devices, exchange(): return lax.all_to_all(array, 'dap', 0, 0, tiled=True)  13 us
    all_to_all x1, starting transfers between devices, exchange(): return lax.all_to_all(array, 'dap', 0, 0, tiled=True)  4.42 us
    pallas_call x1, Pallas kernels, per_device(): call(functools.partial(other_heads_kernel, head_dim), like, scratch, 10,...  4.25 us
    pallas_call x1, Pallas kernels, per_device(): call(functools.partial(own_heads_kernel, head_dim), [like, like, like, wi...  3.96 us
    pallas_call x1, Pallas kernels, per_device(): call(edges_kernel, shape((hidden, TILE, total), BF16), [tall], 4, limit=E...  3.78 us
    pallas_call x1, Pallas kernels, per_device(): call(product_kernel, shape((devices, TILE, total // 2), BF16), [tall, squ...  1.98 us
  transfers between devices with their start and end apart: 2, of which 1 were waited for; matrix products, arithmetic and copies ran while one was open for 0% of the time, Pallas kernels for 5%

profile of v3, /device:TPU:1, one launch (start us, length us, event | category | flops | bytes accessed | tf_op | source)
XLA Modules:
  0.0 89.3 jit_solution(2924938173883646236)
XLA Ops:
  0.0 3.8 %shard_map.91 = bf16[128,8,512]{2,1,0:T(8,128)(2,1)} custom-call(bf16[4,512,128]{2,1,0:T(8,128)(2,1)} %pair_ref.5, s32[4,512]{1,0:T(4,128)} %mask_ref.3, f32[3,128]{1,0:T(4,128)} %gains_ref.5, bf16[128,512]{1,0:T(8,128)(2,1)} %w_ref.1), custom_call_target="tpu_custom_call" | custom-call | tf_op jit(solution)/shard_map/pallas_call | solution.py:272
  3.8 30.8 %all_to_all.15.sides_ref = bf16[128,8,512]{2,1,0:T(8,128)(2,1)S(1)} all-to-all(bf16[128,8,512]{2,1,0:T(8,128)(2,1)} %shard_map.91), channel_id=1, replica_groups=mesh['dap'=128] {'dap'}, dimensions={0} | all-to-all | bytes 2097152 | tf_op jit(solution)/shard_map/all_to_all | solution.py:255
  34.6 2.0 %shard_map.92 = bf16[128,8,256]{2,1,0:T(8,128)(2,1)} custom-call(bf16[128,8,512]{2,1,0:T(8,128)(2,1)S(1)} %all_to_all.15.sides_ref), custom_call_target="tpu_custom_call" | custom-call | tf_op jit(solution)/shard_map/pallas_call | solution.py:276
  36.6 0.0 copy-start
  36.6 0.0 copy-start.5
  36.6 0.0 copy-start.6
  36.6 4.4 %all-to-all-start.1 = ((bf16[128,8,256]{2,1,0:T(8,128)(2,1)}), bf16[128,8,256]{2,1,0:T(8,128)(2,1)S(1)}, u32[]{:S(2)}, u32[]{:S(2)}) async-start(bf16[128,8,256]{2,1,0:T(8,128)(2,1)} %shard_map.92), calls=%async_computation.1 | async-start | bytes 1048576 | tf_op jit(solution)/shard_map/all_to_all | solution.py:255
  41.0 0.0 copy-done
  41.0 0.0 copy-done.5
  41.1 0.0 copy-done.6
  41.1 0.0 copy-start.2
  41.1 0.0 copy-start.4
  41.1 0.8 shard_map.93.gate_ref
  41.9 0.0 copy-start.7
  41.9 13.0 %all-to-all-done.1.prod_ref = bf16[128,8,256]{2,1,0:T(8,128)(2,1)S(1)} async-done(((bf16[128,8,256]{2,1,0:T(8,128)(2,1)}), bf16[128,8,256]{2,1,0:T(8,128)(2,1)S(1)}, u32[]{:S(2)}, u32[]{:S(2)}) %all-to-all-start.1) | async-done | bytes 524320 | tf_op jit(solution)/shard_map/all_to_all | solution.py:255
  54.9 0.0 copy-done.2
  54.9 0.0 copy-done.4
  54.9 0.0 copy-done.7
  54.9 1.4 %shard_map.94 = (bf16[4,512,128]{2,1,0:T(8,128)(2,1)S(1)}, bf16[4,512,128]{2,1,0:T(8,128)(2,1)S(1)}, f32[4,512]{1,0:T(4,128)S(1)}, bf16[128,8,512]{2,1,0:T(8,128)(2,1)S(1)}) custom-call(bf16[128,8,256]{2,1,0:T(8,128)(2,1)S(1)} %all-to-all-done.1.prod_ref, bf16[4,512,128]{2,1,0:T(8,128)(2,1)S(1)} %copy-done, f32[4,512,128]{2,1,0:T(8,128)S(1)} %shard_map.93.gate_ref, ...), custom_call_target="tpu_custom_call" | custom-call | tf_op jit(solution)/shard_map/pallas_call | solution.py:289
  56.3 0.0 copy-start.1
  56.3 23.7 %all_to_all.16.bias_ref = bf16[128,8,512]{2,1,0:T(8,128)(2,1)S(1)} all-to-all(bf16[128,8,512]{2,1,0:T(8,128)(2,1)S(1)} %get-tuple-element.15), channel_id=1, replica_groups=mesh['dap'=128] {'dap'}, dimensions={0} | all-to-all | bytes 2097152 | tf_op jit(solution)/shard_map/all_to_all | solution.py:255
  80.0 0.9 collective-permute-start
  80.9 0.0 copy-done.1
  80.9 0.0 copy-start.3
  80.9 4.0 %shard_map.95 = (bf16[4,512,128]{2,1,0:T(8,128)(2,1)S(1)}, bf16[4,512,128]{2,1,0:T(8,128)(2,1)S(1)}, bf16[4,512,128]{2,1,0:T(8,128)(2,1)S(1)}, f32[4,512,128]{2,1,0:T(8,128)S(1)}, bf16[4,512,128]{2,1,0:T(8,128)(2,1)S(1)}) custom-call(s32[1]{0:T(128)} %bitcast.1.first_head, bf16[4,512,128]{2,1,0:T(8,128)(2,1)S(1)} %get-tuple-element.14.normed_ref, ...), custom_call_target="tpu_custom_call" | custom-call | tf_op jit(solution)/shard_map/pallas_call | solution.py:302
  84.8 0.0 collective-permute-done.bias_ref
  84.9 0.0 copy-done.3
  84.9 4.2 %shard_map.96 = bf16[4,512,128]{2,1,0:T(8,128)(2,1)} custom-call(s32[1]{0:T(128)} %bitcast.first_head, bf16[4,512,128]{2,1,0:T(8,128)(2,1)S(1)} %get-tuple-element.17.query_ref, bf16[4,512,128]{2,1,0:T(8,128)(2,1)S(1)} %get-tuple-element.18.key_ref, bf16[4,512,128]{2,1,0:T(8,128)(2,1)S(1)} %get-tuple-element.19.value_ref, ...), custom_call_target="tpu_custom_call" | custom-call | tf_op jit(solution)/shard_map/pallas_call | solution.py:310
Async XLA Ops:
  36.6 4.4 %copy-start = (bf16[4,512,128]{2,1,0:T(8,128)(2,1)S(1)}, bf16[4,512,128]{2,1,0:T(8,128)(2,1)}, u32[]{:S(2)}) copy-start(bf16[4,512,128]{2,1,0:T(8,128)(2,1)} %pair_ref.5) | copy-start | bytes 1572868
  36.6 4.4 %copy-start.5 = (bf16[128,128]{1,0:T(8,128)(2,1)S(1)}, bf16[128,128]{1,0:T(8,128)(2,1)}, u32[]{:S(2)}) copy-start(bf16[128,128]{1,0:T(8,128)(2,1)} %wg_ref.1) | copy-start | bytes 98308
  36.6 4.5 %copy-start.6 = (f32[3,128]{1,0:T(4,128)S(1)}, f32[3,128]{1,0:T(4,128)}, u32[]{:S(2)}) copy-start(f32[3,128]{1,0:T(4,128)} %gains_ref.5) | copy-start | bytes 4612
  36.6 18.3 %all-to-all-start.1 = ((bf16[128,8,256]{2,1,0:T(8,128)(2,1)}), bf16[128,8,256]{2,1,0:T(8,128)(2,1)S(1)}, u32[]{:S(2)}, u32[]{:S(2)}) async-start(bf16[128,8,256]{2,1,0:T(8,128)(2,1)} %shard_map.92), calls=%async_computation.1 | async-start | bytes 1048576 | tf_op jit(solution)/shard_map/all_to_all | solution.py:255
  41.1 13.8 %copy-start.2 = (bf16[128,128]{1,0:T(8,128)(2,1)S(1)}, bf16[128,128]{1,0:T(8,128)(2,1)}, u32[]{:S(2)}) copy-start(bf16[128,128]{1,0:T(8,128)(2,1)} %wo_ref.1) | copy-start | bytes 98308
  41.1 13.8 %copy-start.4 = (s32[4,512]{1,0:T(4,128)S(1)}, s32[4,512]{1,0:T(4,128)}, u32[]{:S(2)}) copy-start(s32[4,512]{1,0:T(4,128)} %mask_ref.3) | copy-start | bytes 24580
  41.9 13.0 %copy-start.7 = (bf16[128,4]{0,1:T(4,128)(2,1)S(1)}, bf16[128,4]{0,1:T(4,128)(2,1)}, u32[]{:S(2)}) copy-start(bf16[128,4]{0,1:T(4,128)(2,1)} %param.16) | copy-start | bytes 3076
  56.3 24.6 %copy-start.1 = (bf16[128,512]{1,0:T(8,128)(2,1)S(1)}, bf16[128,512]{1,0:T(8,128)(2,1)}, u32[]{:S(2)}) copy-start(bf16[128,512]{1,0:T(8,128)(2,1)} %win_ref.1) | copy-start | bytes 393220
  80.0 4.8 %collective-permute-start = (bf16[128,8,512]{2,1,0:T(8,128)(2,1)S(1)}, bf16[128,8,512]{2,1,0:T(8,128)(2,1)S(1)}, u32[]{:S(2)}, u32[]{:S(2)}) collective-permute-start(bf16[128,8,512]{2,1,0:T(8,128)(2,1)S(1)} %all_to_all.16.bias_ref), channel_id=1, source_target_pairs={{0,1},{1,0},{2,3},{3,2},{4,5},{5,4},{6,7},{7,6},{8,9},{9,8},{10,11... | collective-permute-start | bytes 3145736 | tf_op jit(solution)/shard_map/ppermute | solution.py:297
  80.9 4.0 %copy-start.3 = (bf16[128,128]{1,0:T(8,128)(2,1)S(1)}, bf16[128,128]{1,0:T(8,128)(2,1)}, u32[]{:S(2)}) copy-start(bf16[128,128]{1,0:T(8,128)(2,1)} %wout_ref.1) | copy-start | bytes 98308

commit v4 on v3

--- a/solution.py
+++ b/solution.py
@@ -14,6 +14,7 @@
 EDGES_LIMIT = 60 * 1024 * 1024
 LOG2E = math.log2(math.e)
 TILE = 8
+MASK_AT, GAIN_AT, BIAS_AT, SMALL = 0, 8, 16, 24
 
 
 def dot(a, b, ca, cb):
@@ -25,10 +26,14 @@
 
 
 def norm_rows(values, gain):
-    mean = jnp.mean(values, axis=-1, keepdims=True)
-    centered = values - mean
-    var = jnp.mean(centered * centered, axis=-1, keepdims=True)
-    return centered * lax.rsqrt(var + 1e-05) * gain
+    size = values.shape[-1]
+    row = lax.broadcasted_iota(jnp.int32, (size, size), 0)
+    col = lax.broadcasted_iota(jnp.int32, (size, size), 1)
+    centering = ((row == col).astype(F32) - 1.0 / size).astype(BF16)
+    average = jnp.full((size, size), 1.0 / size, BF16)
+    centered = dot(values, centering, 1, 0)
+    var = dot((centered * centered).astype(BF16), average, 1, 0)
+    return (centered * lax.rsqrt(var + 1e-05) * gain).astype(BF16)
 
 
 def put_rows(scratch, start, stride, values):
@@ -54,11 +59,17 @@
         out_ref[:, :, lane * 128 : (lane + 1) * 128] = part.astype(BF16)
 
 
-def edges_kernel(pair_ref, mask_ref, gains_ref, w_ref, out_ref, scratch):
+def edges_kernel(pair_ref, mask_ref, gains_ref, w_ref, wg_ref, wb_ref, out_ref, gate_ref, small_ref, scratch):
     rows, total = mask_ref.shape
+    width = gains_ref.shape[1]
+    small_ref[MASK_AT : MASK_AT + rows, :] = (1000000000.0 * LOG2E) * (mask_ref[...].astype(F32) - 1.0)
+    small_ref[GAIN_AT : GAIN_AT + 3, 0:width] = gains_ref[...]
+    small_ref[BIAS_AT : BIAS_AT + wb_ref.shape[0], 0:width] = wb_ref[...].astype(F32)
     hidden = out_ref.shape[0]
-    normed = [norm_rows(pair_ref[row].astype(F32), gains_ref[0:1, :]).astype(BF16) for row in range(rows)]
+    normed = [norm_rows(pair_ref[row], gains_ref[0:1, :]) for row in range(rows)]
     edges = [dot(w_ref[...], normed[row], 0, 1) for row in range(rows)]
+    for row in range(rows):
+        gate_ref[row] = sigmoid(dot(normed[row], wg_ref[...], 1, 0))
     for row in range(rows):
         mask = mask_ref[row : row + 1, :].astype(F32)
         for side in range(2):
@@ -77,40 +88,31 @@
         put_rows(right_ref, row, rows, get_rows(scratch, rows + row, devices, TILE))
     right = jnp.concatenate([right_ref[lane] for lane in range(total // 128)], axis=1).astype(BF16)
     left = [get_rows(scratch, row, devices, TILE).astype(BF16) for row in range(rows)]
-    product = [dot(left[row], right, 1, 1) for row in range(rows)]
+    product = dot(jnp.concatenate(left, axis=0), right, 1, 1)
     for row in range(rows):
         for part in range(2):
-            put_rows(prod_ref, 2 * row + part, TILE, product[row][:, part * half : (part + 1) * half])
+            put_rows(prod_ref, 2 * row + part, TILE, product[row * devices : (row + 1) * devices, part * half : (part + 1) * half])
     fill(out_ref, prod_ref)
-
-
-def gate_kernel(pair_ref, gains_ref, wg_ref, out_ref):
-    for row in range(pair_ref.shape[0]):
-        normed = norm_rows(pair_ref[row].astype(F32), gains_ref[0:1, :]).astype(BF16)
-        out_ref[row] = sigmoid(dot(normed, wg_ref[...], 1, 0))
 
 
 def middle_kernel(
     prod_ref,
     pair_ref,
     gate_ref,
-    gains_ref,
-    mask_ref,
+    small_ref,
     wo_ref,
-    wb_ref,
     mid_ref,
     normed_ref,
-    masked_ref,
     bias_ref,
     scratch,
     bias_f,
 ):
     rows, total, width = pair_ref.shape
-    heads = wb_ref.shape[0]
+    heads = 2 * TILE // rows
     devices = bias_ref.shape[0]
     spill(scratch, prod_ref[...])
-    gain = gains_ref[1:2, :].T
-    masked_ref[...] = (1000000000.0 * LOG2E) * (mask_ref[...].astype(F32) - 1.0)
+    gain = small_ref[GAIN_AT + 1 : GAIN_AT + 2, 0:width].T
+    wb = small_ref[BIAS_AT : BIAS_AT + heads, 0:width].astype(BF16)
     prod_normed = []
     for row in range(rows):
         prod = jnp.concatenate(
@@ -125,9 +127,9 @@
     mid_normed = []
     for row in range(rows):
         mid_ref[row] = mid[row]
-        mid_normed.append(norm_rows(mid[row].astype(F32), gains_ref[2:3, :]).astype(BF16))
+        mid_normed.append(norm_rows(mid[row], small_ref[GAIN_AT + 2 : GAIN_AT + 3, 0:width]))
         normed_ref[row] = mid_normed[row]
-    bias = [dot(wb_ref[...], mid_normed[row], 1, 1) for row in range(rows)]
+    bias = [dot(wb, mid_normed[row], 1, 1) for row in range(rows)]
     for row in range(rows):
         for head in range(heads):
             bias_f[head * rows + row : head * rows + row + 1, :] = bias[row][head : head + 1, :]
@@ -137,7 +139,7 @@
             bias_ref[2 * pair_of + part] = block
 
 
-def attend(head_dim, first_head, query_ref, key_ref, value_ref, gate_ref, bias_ref, masked_ref, scratch, bias_f):
+def attend(head_dim, first_head, query_ref, key_ref, value_ref, gate_ref, bias_ref, small_ref, scratch, bias_f):
     rows, total, width = value_ref.shape
     devices = bias_ref.shape[0]
     own = TILE // rows
@@ -155,7 +157,7 @@
         for head in range(own):
             pick = (lane_head == base + head).astype(BF16)
             bias = jnp.concatenate([bias_f[head, lane] for lane in range(total // 128)], axis=1)
-            logits = dot(query_ref[row] * pick, key_ref[row], 1, 1) + bias + masked_ref[row : row + 1, :]
+            logits = dot(query_ref[row] * pick, key_ref[row], 1, 1) + bias + small_ref[MASK_AT + row : MASK_AT + row + 1, :]
             top = jnp.max(logits, axis=-1, keepdims=True)
             expos.append(jnp.exp2(logits - top).astype(BF16))
             value = value_ref[row]
@@ -173,7 +175,7 @@
     first_head,
     normed_ref,
     bias_ref,
-    masked_ref,
+    small_ref,
     win_ref,
     query_ref,
     key_ref,
@@ -192,7 +194,7 @@
         value_ref[row] = packed[row][:, 2 * width : 3 * width].astype(BF16)
         gate_ref[row] = sigmoid(packed[row][:, 3 * width : 4 * width])
     attended = attend(
-        head_dim, first_head, query_ref, key_ref, value_ref, gate_ref, bias_ref, masked_ref, scratch, bias_f
+        head_dim, first_head, query_ref, key_ref, value_ref, gate_ref, bias_ref, small_ref, scratch, bias_f
     )
     for row in range(rows):
         out_ref[row] = attended[row]
@@ -206,7 +208,7 @@
     value_ref,
     gate_ref,
     bias_ref,
-    masked_ref,
+    small_ref,
     mid_ref,
     part_ref,
     wout_ref,
@@ -218,7 +220,7 @@
 ):
     rows = mid_ref.shape[0]
     attended = attend(
-        head_dim, first_head, query_ref, key_ref, value_ref, gate_ref, bias_ref, masked_ref, scratch, bias_f
+        head_dim, first_head, query_ref, key_ref, value_ref, gate_ref, bias_ref, small_ref, scratch, bias_f
     )
     copies = []
     for row in range(rows):
@@ -230,7 +232,7 @@
         copy.wait()
 
 
-def call(kernel, out_shape, scratch, n_args, scalars=0, limit=VMEM_LIMIT, out_space=pltpu.VMEM, cost=None):
+def call(kernel, out_shape, scratch, n_args, scalars=0, limit=VMEM_LIMIT, out_space=pltpu.VMEM):
     specs = [
         pl.BlockSpec(memory_space=pltpu.SMEM if at < scalars else pltpu.VMEM) for at in range(n_args)
     ]
@@ -241,13 +243,6 @@
         out_shape=out_shape,
         scratch_shapes=scratch,
         compiler_params=pltpu.CompilerParams(vmem_limit_bytes=limit),
-        cost_estimate=cost,
-    )
-
-
-def cost(flops, bytes_accessed, transcendentals):
-    return pl.CostEstimate(
-        flops=flops, bytes_accessed=bytes_accessed, transcendentals=transcendentals
     )
 
 
@@ -269,29 +264,30 @@
     tall = pltpu.VMEM((lanes, devices * TILE, 128), F32)
     square = pltpu.VMEM((lanes, total, 128), F32)
     short = pltpu.VMEM((lanes // 2, devices * TILE, 128), F32)
-    sides = call(
-        edges_kernel, shape((hidden, TILE, total), BF16), [tall], 4, limit=EDGES_LIMIT
-    )(pair, pair_mask, norm_gains, w_edges)
+    sides, gate, small = call(
+        edges_kernel,
+        [
+            shape((hidden, TILE, total), BF16),
+            shape((rows, total, width), F32),
+            shape((SMALL, total), F32),
+        ],
+        [tall],
+        6,
+        limit=EDGES_LIMIT,
+    )(pair, pair_mask, norm_gains, w_edges, w_tri_gate, w_tri_bias.T)
     sides = exchange(sides)
     product = call(
         product_kernel, shape((devices, TILE, total // 2), BF16), [tall, square, short], 1
     )(sides)
     product = exchange(product)
-    gate = call(
-        gate_kernel,
-        shape((rows, total, width), F32),
-        [],
-        3,
-        cost=cost(2 * rows * total * width * width, 4 << 20, rows * total * width),
-    )(pair, norm_gains, w_tri_gate)
     like = shape((rows, total, width), BF16)
     wide = shape((rows, total, width), F32)
-    mid, mid_normed, masked, bias = call(
+    mid, mid_normed, bias = call(
         middle_kernel,
-        [like, like, shape((rows, total), F32), shape((devices, TILE, total), BF16)],
+        [like, like, shape((devices, TILE, total), BF16)],
         [short, pltpu.VMEM((2 * TILE, total), F32)],
-        7,
-    )(product, pair, gate, norm_gains, pair_mask, w_tri_out, w_tri_bias.T)
+        5,
+    )(product, pair, gate, small, w_tri_out)
     mine = exchange(bias)
     swap = [(d, d ^ 1) for d in range(devices)]
     other = lax.ppermute(mine, "dap", swap)
@@ -305,7 +301,7 @@
         scratch,
         5,
         1,
-    )(mine_first, mid_normed, mine, masked, w_attn_in)
+    )(mine_first, mid_normed, mine, small, w_attn_in)
     scratch = scratch + [pltpu.VMEM((rows, total, width), BF16), pltpu.SemaphoreType.DMA((rows,))]
     return call(
         functools.partial(other_heads_kernel, head_dim),
@@ -314,7 +310,7 @@
         10,
         1,
         out_space=pl.ANY,
-    )(other_first, query, key, value, att_gate, other, masked, mid, part, w_attn_out)
+    )(other_first, query, key, value, att_gate, other, small, mid, part, w_attn_out)
 
 
 def solution(mesh):

time: 89.5 us -> 88.1 us (0.984)
  blocking collectives: 54.5 us -> 72.4 us
  waiting for transfers between devices: 13 us -> 0.01 us
  starting transfers between devices: 5.29 us -> 0.87 us
  Pallas kernels: 16.2 us -> 14.3 us
    all_to_all x2 -> x3, blocking collectives: 54.5 us -> 72.4 us  [exchange(): return lax.all_to_all(array, 'dap', 0, 0, tiled=True)]
    all_to_all x1 -> x0, waiting for transfers between devices: 13 us -> none  [exchange(): return lax.all_to_all(array, 'dap', 0, 0, tiled=True)]
    all_to_all x1 -> x0, starting transfers between devices: 4.42 us -> none  [exchange(): return lax.all_to_all(array, 'dap', 0, 0, tiled=True)]
    pallas_call x1, Pallas kernels: 1.98 us -> 0.94 us  [per_device(): call(product_kernel, shape((devices, TILE, total // 2), BF16), [tall, squ...]
    pallas_call x3 -> x2, Pallas kernels: 5.97 us -> 5.17 us  [the longest x1 3.85 us: per_device(): call(edges_kernel, [shape((hidden, TILE, total), BF16), shape((rows, tota...]
  transfers between devices with their start and end apart: 2 -> 1, of which waited for: 1 -> 0; matrix products, arithmetic and copies ran while one was open for 0% -> 0% of each run, Pallas kernels for 5% -> 5%
where the time goes in v4:
time: 88.1 us; the launch traced here: 87.8 us
  blocking collectives  72.4 us (82%)
  Pallas kernels  14.3 us (16%)
    all_to_all x3, blocking collectives, exchange(): return lax.all_to_all(array, 'dap', 0, 0, tiled=True)  72.4 us
    pallas_call x1, Pallas kernels, per_device(): call(functools.partial(other_heads_kernel, head_dim), like, scratch, 10,...  4.24 us
    pallas_call x1, Pallas kernels, per_device(): call(functools.partial(own_heads_kernel, head_dim), [like, like, like, wi...  3.96 us
    pallas_call x1, Pallas kernels, per_device(): call(edges_kernel, [shape((hidden, TILE, total), BF16), shape((rows, tota...  3.85 us
  transfers between devices with their start and end apart: 1, of which 0 were waited for; matrix products, arithmetic and copies ran while one was open for 0% of the time, Pallas kernels for 5%

profile of v4, /device:TPU:1, one launch (start us, length us, event | category | flops | bytes accessed | tf_op | source)
XLA Modules:
  0.0 87.8 jit_solution(14179096153483821697)
XLA Ops:
  0.0 3.8 %shard_map.91 = (bf16[128,8,512]{2,1,0:T(8,128)(2,1)}, f32[4,512,128]{2,1,0:T(8,128)}, f32[24,512]{1,0:T(8,128)}) custom-call(bf16[4,512,128]{2,1,0:T(8,128)(2,1)} %pair_ref.3, s32[4,512]{1,0:T(4,128)} %mask_ref.1, f32[3,128]{1,0:T(4,128)} %gains_ref.1, bf16[128,512]{1,0:T(8,128)(2,1)} %w_ref.1, bf16[128,128]{1,0:T(8,128)(2,1)} %wg_ref.1, bf16[4,128]{1,0:T(4,128)(2,1)} %bitcast.3), custom_call_target="tpu_custom_call" | custom-call | tf_op jit(solution)/shard_map/pallas_call | solution.py:267
  3.8 30.8 %all_to_all.15.sides_ref = bf16[128,8,512]{2,1,0:T(8,128)(2,1)S(1)} all-to-all(bf16[128,8,512]{2,1,0:T(8,128)(2,1)} %get-tuple-element.16), channel_id=1, replica_groups=mesh['dap'=128] {'dap'}, dimensions={0} | all-to-all | bytes 2097152 | tf_op jit(solution)/shard_map/all_to_all | solution.py:250
  34.7 0.0 copy-start.1
  34.7 0.9 %shard_map.92 = bf16[128,8,256]{2,1,0:T(8,128)(2,1)S(1)} custom-call(bf16[128,8,512]{2,1,0:T(8,128)(2,1)S(1)} %all_to_all.15.sides_ref), custom_call_target="tpu_custom_call" | custom-call | tf_op jit(solution)/shard_map/pallas_call | solution.py:279
  35.6 0.0 copy-start
  35.7 0.0 copy-start.2
  35.7 0.0 copy-start.4
  35.7 17.9 %all_to_all.16.prod_ref = bf16[128,8,256]{2,1,0:T(8,128)(2,1)S(1)} all-to-all(bf16[128,8,256]{2,1,0:T(8,128)(2,1)S(1)} %shard_map.92), channel_id=1, replica_groups=mesh['dap'=128] {'dap'}, dimensions={0} | all-to-all | bytes 1048576 | tf_op jit(solution)/shard_map/all_to_all | solution.py:250
  53.5 0.0 copy-done.1
  53.6 0.0 copy-done
  53.6 0.0 copy-done.2
  53.6 0.0 copy-done.4
  53.6 1.3 %shard_map.93 = (bf16[4,512,128]{2,1,0:T(8,128)(2,1)S(1)}, bf16[4,512,128]{2,1,0:T(8,128)(2,1)S(1)}, bf16[128,8,512]{2,1,0:T(8,128)(2,1)S(1)}) custom-call(bf16[128,8,256]{2,1,0:T(8,128)(2,1)S(1)} %all_to_all.16.prod_ref, bf16[4,512,128]{2,1,0:T(8,128)(2,1)S(1)} %copy-done, f32[4,512,128]{2,1,0:T(8,128)S(1)} %copy-done.1, f32[24,512]{1,0:T(8,128)S(1)} %copy-done.2, ...), custom_call_target="tpu_custom_call" | custom-call | tf_op jit(solution)/shard_map/pallas_call | solution.py:285
  54.9 0.0 copy-start.3
  54.9 23.7 %all_to_all.17.bias_ref = bf16[128,8,512]{2,1,0:T(8,128)(2,1)S(1)} all-to-all(bf16[128,8,512]{2,1,0:T(8,128)(2,1)S(1)} %get-tuple-element.20), channel_id=1, replica_groups=mesh['dap'=128] {'dap'}, dimensions={0} | all-to-all | bytes 2097152 | tf_op jit(solution)/shard_map/all_to_all | solution.py:250
  78.6 0.9 collective-permute-start
  79.5 0.0 copy-done.3
  79.5 0.0 copy-start.5
  79.5 4.0 %shard_map.94 = (bf16[4,512,128]{2,1,0:T(8,128)(2,1)S(1)}, bf16[4,512,128]{2,1,0:T(8,128)(2,1)S(1)}, bf16[4,512,128]{2,1,0:T(8,128)(2,1)S(1)}, f32[4,512,128]{2,1,0:T(8,128)S(1)}, bf16[4,512,128]{2,1,0:T(8,128)(2,1)S(1)}) custom-call(s32[1]{0:T(128)} %bitcast.1.first_head, bf16[4,512,128]{2,1,0:T(8,128)(2,1)S(1)} %get-tuple-element.19.normed_ref, ...), custom_call_target="tpu_custom_call" | custom-call | tf_op jit(solution)/shard_map/pallas_call | solution.py:298
  83.4 0.0 collective-permute-done.bias_ref
  83.4 0.0 copy-done.5
  83.4 4.2 %shard_map.95 = bf16[4,512,128]{2,1,0:T(8,128)(2,1)} custom-call(s32[1]{0:T(128)} %bitcast.first_head, bf16[4,512,128]{2,1,0:T(8,128)(2,1)S(1)} %get-tuple-element.21.query_ref, bf16[4,512,128]{2,1,0:T(8,128)(2,1)S(1)} %get-tuple-element.22.key_ref, bf16[4,512,128]{2,1,0:T(8,128)(2,1)S(1)} %get-tuple-element.23.value_ref, ...), custom_call_target="tpu_custom_call" | custom-call | tf_op jit(solution)/shard_map/pallas_call | solution.py:306
Async XLA Ops:
  34.7 18.9 %copy-start.1 = (f32[4,512,128]{2,1,0:T(8,128)S(1)}, f32[4,512,128]{2,1,0:T(8,128)}, u32[]{:S(2)}) copy-start(f32[4,512,128]{2,1,0:T(8,128)} %get-tuple-element.17.gate_ref) | copy-start | bytes 3145732
  35.6 17.9 %copy-start = (bf16[4,512,128]{2,1,0:T(8,128)(2,1)S(1)}, bf16[4,512,128]{2,1,0:T(8,128)(2,1)}, u32[]{:S(2)}) copy-start(bf16[4,512,128]{2,1,0:T(8,128)(2,1)} %pair_ref.3) | copy-start | bytes 1572868
  35.7 17.9 %copy-start.2 = (f32[24,512]{1,0:T(8,128)S(1)}, f32[24,512]{1,0:T(8,128)}, u32[]{:S(2)}) copy-start(f32[24,512]{1,0:T(8,128)} %get-tuple-element.18.small_ref) | copy-start | bytes 147460
  35.7 17.9 %copy-start.4 = (bf16[128,128]{1,0:T(8,128)(2,1)S(1)}, bf16[128,128]{1,0:T(8,128)(2,1)}, u32[]{:S(2)}) copy-start(bf16[128,128]{1,0:T(8,128)(2,1)} %wo_ref.1) | copy-start | bytes 98308
  54.9 24.6 %copy-start.3 = (bf16[128,512]{1,0:T(8,128)(2,1)S(1)}, bf16[128,512]{1,0:T(8,128)(2,1)}, u32[]{:S(2)}) copy-start(bf16[128,512]{1,0:T(8,128)(2,1)} %win_ref.1) | copy-start | bytes 393220
  78.6 4.8 %collective-permute-start = (bf16[128,8,512]{2,1,0:T(8,128)(2,1)S(1)}, bf16[128,8,512]{2,1,0:T(8,128)(2,1)S(1)}, u32[]{:S(2)}, u32[]{:S(2)}) collective-permute-start(bf16[128,8,512]{2,1,0:T(8,128)(2,1)S(1)} %all_to_all.17.bias_ref), channel_id=1, source_target_pairs={{0,1},{1,0},{2,3},{3,2},{4,5},{5,4},{6,7},{7,6},{8,9},{9,8},{10,11... | collective-permute-start | bytes 3145736 | tf_op jit(solution)/shard_map/ppermute | solution.py:293
  79.5 4.0 %copy-start.5 = (bf16[128,128]{1,0:T(8,128)(2,1)S(1)}, bf16[128,128]{1,0:T(8,128)(2,1)}, u32[]{:S(2)}) copy-start(bf16[128,128]{1,0:T(8,128)(2,1)} %wout_ref.1) | copy-start | bytes 98308

commit v5 on v4

--- a/solution.py
+++ b/solution.py
@@ -59,17 +59,11 @@
         out_ref[:, :, lane * 128 : (lane + 1) * 128] = part.astype(BF16)
 
 
-def edges_kernel(pair_ref, mask_ref, gains_ref, w_ref, wg_ref, wb_ref, out_ref, gate_ref, small_ref, scratch):
+def edges_kernel(pair_ref, mask_ref, gains_ref, w_ref, out_ref, scratch):
     rows, total = mask_ref.shape
-    width = gains_ref.shape[1]
-    small_ref[MASK_AT : MASK_AT + rows, :] = (1000000000.0 * LOG2E) * (mask_ref[...].astype(F32) - 1.0)
-    small_ref[GAIN_AT : GAIN_AT + 3, 0:width] = gains_ref[...]
-    small_ref[BIAS_AT : BIAS_AT + wb_ref.shape[0], 0:width] = wb_ref[...].astype(F32)
     hidden = out_ref.shape[0]
     normed = [norm_rows(pair_ref[row], gains_ref[0:1, :]) for row in range(rows)]
     edges = [dot(w_ref[...], normed[row], 0, 1) for row in range(rows)]
-    for row in range(rows):
-        gate_ref[row] = sigmoid(dot(normed[row], wg_ref[...], 1, 0))
     for row in range(rows):
         mask = mask_ref[row : row + 1, :].astype(F32)
         for side in range(2):
@@ -77,6 +71,17 @@
             value = edges[row][(2 * side + 1) * hidden : (2 * side + 2) * hidden]
             put_rows(scratch, side * rows + row, TILE, mask * sigmoid(gate) * value)
     fill(out_ref, scratch)
+
+
+def gate_kernel(pair_ref, mask_ref, gains_ref, wg_ref, wb_ref, gate_ref, small_ref):
+    rows = mask_ref.shape[0]
+    width = gains_ref.shape[1]
+    small_ref[MASK_AT : MASK_AT + rows, :] = (1000000000.0 * LOG2E) * (mask_ref[...].astype(F32) - 1.0)
+    small_ref[GAIN_AT : GAIN_AT + 3, 0:width] = gains_ref[...]
+    small_ref[BIAS_AT : BIAS_AT + wb_ref.shape[0], 0:width] = wb_ref[...].astype(F32)
+    normed = [norm_rows(pair_ref[row], gains_ref[0:1, :]) for row in range(rows)]
+    for row in range(rows):
+        gate_ref[row] = sigmoid(dot(normed[row], wg_ref[...], 1, 0))
 
 
 def product_kernel(sides_ref, out_ref, scratch, right_ref, prod_ref):
@@ -232,7 +237,7 @@
         copy.wait()
 
 
-def call(kernel, out_shape, scratch, n_args, scalars=0, limit=VMEM_LIMIT, out_space=pltpu.VMEM):
+def call(kernel, out_shape, scratch, n_args, scalars=0, limit=VMEM_LIMIT, out_space=pltpu.VMEM, cost=None):
     specs = [
         pl.BlockSpec(memory_space=pltpu.SMEM if at < scalars else pltpu.VMEM) for at in range(n_args)
     ]
@@ -243,6 +248,7 @@
         out_shape=out_shape,
         scratch_shapes=scratch,
         compiler_params=pltpu.CompilerParams(vmem_limit_bytes=limit),
+        cost_estimate=cost,
     )
 
 
@@ -264,18 +270,22 @@
     tall = pltpu.VMEM((lanes, devices * TILE, 128), F32)
     square = pltpu.VMEM((lanes, total, 128), F32)
     short = pltpu.VMEM((lanes // 2, devices * TILE, 128), F32)
-    sides, gate, small = call(
-        edges_kernel,
-        [
-            shape((hidden, TILE, total), BF16),
-            shape((rows, total, width), F32),
-            shape((SMALL, total), F32),
-        ],
-        [tall],
-        6,
-        limit=EDGES_LIMIT,
-    )(pair, pair_mask, norm_gains, w_edges, w_tri_gate, w_tri_bias.T)
+    sides = call(
+        edges_kernel, shape((hidden, TILE, total), BF16), [tall], 4, limit=EDGES_LIMIT
+    )(pair, pair_mask, norm_gains, w_edges)
+    gate, small = call(
+        gate_kernel,
+        [shape((rows, total, width), F32), shape((SMALL, total), F32)],
+        [],
+        5,
+        cost=pl.CostEstimate(
+            flops=2 * rows * total * width * width,
+            bytes_accessed=4 * rows * total * width,
+            transcendentals=rows * total * width,
+        ),
+    )(pair, pair_mask, norm_gains, w_tri_gate, w_tri_bias.T)
     sides = exchange(sides)
+    sides, gate, small = lax.optimization_barrier((sides, gate, small))
     product = call(
         product_kernel, shape((devices, TILE, total // 2), BF16), [tall, square, short], 1
     )(sides)

time: 88.1 us -> 87.4 us (level)
  blocking collectives: 72.4 us -> 41.5 us
  waiting for transfers between devices: 0.01 us -> 18 us
  starting transfers between devices: 0.87 us -> 12.4 us
    all_to_all x3 -> x2, blocking collectives: 72.4 us -> 41.5 us  [exchange(): return lax.all_to_all(array, 'dap', 0, 0, tiled=True)]
    all_to_all x0 -> x1, waiting for transfers between devices: none -> 18 us  [exchange(): return lax.all_to_all(array, 'dap', 0, 0, tiled=True)]
    all_to_all x0 -> x1, starting transfers between devices: none -> 11.5 us  [exchange(): return lax.all_to_all(array, 'dap', 0, 0, tiled=True)]
    pallas_call x1 -> x2, Pallas kernels: 3.85 us -> 4.07 us  [the longest x1 3.39 us: per_device(): call(edges_kernel, shape((hidden, TILE, total), BF16), [tall], 4, limit=E...]
  transfers between devices with their start and end apart: 1 -> 2, of which waited for: 0 -> 1; matrix products, arithmetic and copies ran while one was open for 0% -> 0% of each run, Pallas kernels for 5% -> 5%
where the time goes in v5:
time: 87.4 us; the launch traced here: 87.1 us
  blocking collectives  41.5 us (47%)
  waiting for transfers between devices  18 us (21%)
  Pallas kernels  14.3 us (16%)
  starting transfers between devices  12.4 us (14%)
    all_to_all x2, blocking collectives, exchange(): return lax.all_to_all(array, 'dap', 0, 0, tiled=True)  41.5 us
    all_to_all x1, waiting for transfers between devices, exchange(): return lax.all_to_all(array, 'dap', 0, 0, tiled=True)  18 us
    all_to_all x1, starting transfers between devices, exchange(): return lax.all_to_all(array, 'dap', 0, 0, tiled=True)  11.5 us
    pallas_call x1, Pallas kernels, per_device(): call(functools.partial(other_heads_kernel, head_dim), like, scratch, 10,...  4.09 us
    pallas_call x1, Pallas kernels, per_device(): call(functools.partial(own_heads_kernel, head_dim), [like, like, like, wi...  3.85 us
    pallas_call x1, Pallas kernels, per_device(): call(edges_kernel, shape((hidden, TILE, total), BF16), [tall], 4, limit=E...  3.39 us
  transfers between devices with their start and end apart: 2, of which 1 were waited for; matrix products, arithmetic and copies ran while one was open for 0% of the time, Pallas kernels for 5%

profile of v5, /device:TPU:1, one launch (start us, length us, event | category | flops | bytes accessed | tf_op | source)
XLA Modules:
  0.0 87.1 jit_solution(8399002641518140813)
XLA Ops:
  0.0 3.4 %shard_map.91 = bf16[128,8,512]{2,1,0:T(8,128)(2,1)} custom-call(bf16[4,512,128]{2,1,0:T(8,128)(2,1)} %pair_ref.5, s32[4,512]{1,0:T(4,128)} %mask_ref.3, f32[3,128]{1,0:T(4,128)} %gains_ref.3, bf16[128,512]{1,0:T(8,128)(2,1)} %w_ref.1), custom_call_target="tpu_custom_call" | custom-call | tf_op jit(solution)/shard_map/pallas_call | solution.py:273
  3.4 0.0 copy-start
  3.4 0.0 copy-start.6
  3.4 0.0 copy-start.7
  3.4 0.0 copy-start.8
  3.4 11.5 %all-to-all-start = ((bf16[128,8,512]{2,1,0:T(8,128)(2,1)}), bf16[128,8,512]{2,1,0:T(8,128)(2,1)S(1)}, u32[]{:S(2)}, u32[]{:S(2)}) async-start(bf16[128,8,512]{2,1,0:T(8,128)(2,1)} %shard_map.91), calls=%async_computation | async-start | bytes 2097152 | tf_op jit(solution)/shard_map/all_to_all | solution.py:256
  14.9 0.0 copy-start.9
  14.9 0.0 copy-done
  14.9 0.0 copy-done.6
  14.9 0.0 copy-done.7
  15.0 0.0 copy-done.8
  15.0 0.6 copy-done.9
  15.6 0.7 shard_map.92
  16.3 18.0 %all-to-all-done.sides_ref = bf16[128,8,512]{2,1,0:T(8,128)(2,1)S(1)} async-done(((bf16[128,8,512]{2,1,0:T(8,128)(2,1)}), bf16[128,8,512]{2,1,0:T(8,128)(2,1)S(1)}, u32[]{:S(2)}, u32[]{:S(2)}) %all-to-all-start) | async-done | bytes 1048608 | tf_op jit(solution)/shard_map/all_to_all | solution.py:256
  34.3 0.9 %shard_map.93 = bf16[128,8,256]{2,1,0:T(8,128)(2,1)S(1)} custom-call(bf16[128,8,512]{2,1,0:T(8,128)(2,1)S(1)} %all-to-all-done.sides_ref), custom_call_target="tpu_custom_call" | custom-call | tf_op jit(solution)/shard_map/pallas_call | solution.py:289
  35.2 0.0 copy-start.4
  35.2 17.9 %all_to_all.15.prod_ref = bf16[128,8,256]{2,1,0:T(8,128)(2,1)S(1)} all-to-all(bf16[128,8,256]{2,1,0:T(8,128)(2,1)S(1)} %shard_map.93), channel_id=1, replica_groups=mesh['dap'=128] {'dap'}, dimensions={0} | all-to-all | bytes 1048576 | tf_op jit(solution)/shard_map/all_to_all | solution.py:256
  53.1 0.0 copy-done.4
  53.1 1.3 %shard_map.94 = (bf16[4,512,128]{2,1,0:T(8,128)(2,1)S(1)}, bf16[4,512,128]{2,1,0:T(8,128)(2,1)S(1)}, bf16[128,8,512]{2,1,0:T(8,128)(2,1)S(1)}) custom-call(bf16[128,8,256]{2,1,0:T(8,128)(2,1)S(1)} %all_to_all.15.prod_ref, bf16[4,512,128]{2,1,0:T(8,128)(2,1)S(1)} %copy-done, f32[4,512,128]{2,1,0:T(8,128)S(1)} %get-tuple-element.21.gate_ref, ...), custom_call_target="tpu_custom_call" | custom-call | tf_op jit(solution)/shard_map/pallas_call | solution.py:295
  54.4 0.0 copy-start.1
  54.4 0.0 copy-start.3
  54.4 23.7 %all_to_all.16.bias_ref = bf16[128,8,512]{2,1,0:T(8,128)(2,1)S(1)} all-to-all(bf16[128,8,512]{2,1,0:T(8,128)(2,1)S(1)} %get-tuple-element.24), channel_id=1, replica_groups=mesh['dap'=128] {'dap'}, dimensions={0} | all-to-all | bytes 2097152 | tf_op jit(solution)/shard_map/all_to_all | solution.py:256
  78.1 0.0 copy-done.1
  78.1 0.9 %collective-permute-start = (bf16[128,8,512]{2,1,0:T(8,128)(2,1)S(1)}, bf16[128,8,512]{2,1,0:T(8,128)(2,1)S(1)}, u32[]{:S(2)}, u32[]{:S(2)}) collective-permute-start(bf16[128,8,512]{2,1,0:T(8,128)(2,1)S(1)} %all_to_all.16.bias_ref), channel_id=1, source_target_pairs={{0,1},{1,0},{2,3},{3,2},{4,5},{5,4},{6,7},{7,6},{8,9},{9,8},{10,11... | collective-permute-start | bytes 3145736 | tf_op jit(solution)/shard_map/ppermute | solution.py:303
  79.0 0.0 copy-done.3
  79.0 0.0 copy-start.2
  79.0 0.0 copy-start.5
  79.0 3.9 %shard_map.95 = (bf16[4,512,128]{2,1,0:T(8,128)(2,1)S(1)}, bf16[4,512,128]{2,1,0:T(8,128)(2,1)S(1)}, bf16[4,512,128]{2,1,0:T(8,128)(2,1)S(1)}, f32[4,512,128]{2,1,0:T(8,128)S(1)}, bf16[4,512,128]{2,1,0:T(8,128)(2,1)S(1)}) custom-call(s32[1]{0:T(128)} %bitcast.1.first_head, bf16[4,512,128]{2,1,0:T(8,128)(2,1)S(1)} %get-tuple-element.23.normed_ref, ...), custom_call_target="tpu_custom_call" | custom-call | tf_op jit(solution)/shard_map/pallas_call | solution.py:308
  82.8 0.0 collective-permute-done.bias_ref
  82.9 0.0 copy-done.2
  82.9 0.0 copy-done.5
  82.9 4.1 %shard_map.96 = bf16[4,512,128]{2,1,0:T(8,128)(2,1)} custom-call(s32[1]{0:T(128)} %bitcast.first_head, bf16[4,512,128]{2,1,0:T(8,128)(2,1)S(1)} %get-tuple-element.25.query_ref, bf16[4,512,128]{2,1,0:T(8,128)(2,1)S(1)} %get-tuple-element.26.key_ref, bf16[4,512,128]{2,1,0:T(8,128)(2,1)S(1)} %get-tuple-element.27.value_ref, ...), custom_call_target="tpu_custom_call" | custom-call | tf_op jit(solution)/shard_map/pallas_call | solution.py:316
Async XLA Ops:
  3.4 11.5 %copy-start = (bf16[4,512,128]{2,1,0:T(8,128)(2,1)S(1)}, bf16[4,512,128]{2,1,0:T(8,128)(2,1)}, u32[]{:S(2)}) copy-start(bf16[4,512,128]{2,1,0:T(8,128)(2,1)} %pair_ref.5) | copy-start | bytes 1572868
  3.4 11.5 %copy-start.6 = (s32[4,512]{1,0:T(4,128)S(1)}, s32[4,512]{1,0:T(4,128)}, u32[]{:S(2)}) copy-start(s32[4,512]{1,0:T(4,128)} %mask_ref.3) | copy-start | bytes 24580
  3.4 11.6 %copy-start.7 = (bf16[128,128]{1,0:T(8,128)(2,1)S(1)}, bf16[128,128]{1,0:T(8,128)(2,1)}, u32[]{:S(2)}) copy-start(bf16[128,128]{1,0:T(8,128)(2,1)} %wg_ref.1) | copy-start | bytes 98308
  3.4 11.6 %copy-start.8 = (f32[3,128]{1,0:T(4,128)S(1)}, f32[3,128]{1,0:T(4,128)}, u32[]{:S(2)}) copy-start(f32[3,128]{1,0:T(4,128)} %gains_ref.3) | copy-start | bytes 4612
  3.4 30.9 %all-to-all-start = ((bf16[128,8,512]{2,1,0:T(8,128)(2,1)}), bf16[128,8,512]{2,1,0:T(8,128)(2,1)S(1)}, u32[]{:S(2)}, u32[]{:S(2)}) async-start(bf16[128,8,512]{2,1,0:T(8,128)(2,1)} %shard_map.91), calls=%async_computation | async-start | bytes 2097152 | tf_op jit(solution)/shard_map/all_to_all | solution.py:256
  14.9 0.7 copy-start.9
  35.2 17.9 %copy-start.4 = (bf16[128,128]{1,0:T(8,128)(2,1)S(1)}, bf16[128,128]{1,0:T(8,128)(2,1)}, u32[]{:S(2)}) copy-start(bf16[128,128]{1,0:T(8,128)(2,1)} %wo_ref.1) | copy-start | bytes 98308
  54.4 23.7 %copy-start.1 = (bf16[4,512,128]{2,1,0:T(8,128)(2,1)}, bf16[4,512,128]{2,1,0:T(8,128)(2,1)S(1)}, u32[]{:S(2)}) copy-start(bf16[4,512,128]{2,1,0:T(8,128)(2,1)S(1)} %get-tuple-element.29.mid_ref) | copy-start | bytes 1572868
  54.4 24.6 %copy-start.3 = (bf16[128,512]{1,0:T(8,128)(2,1)S(1)}, bf16[128,512]{1,0:T(8,128)(2,1)}, u32[]{:S(2)}) copy-start(bf16[128,512]{1,0:T(8,128)(2,1)} %win_ref.1) | copy-start | bytes 393220
  78.1 4.7 %collective-permute-start = (bf16[128,8,512]{2,1,0:T(8,128)(2,1)S(1)}, bf16[128,8,512]{2,1,0:T(8,128)(2,1)S(1)}, u32[]{:S(2)}, u32[]{:S(2)}) collective-permute-start(bf16[128,8,512]{2,1,0:T(8,128)(2,1)S(1)} %all_to_all.16.bias_ref), channel_id=1, source_target_pairs={{0,1},{1,0},{2,3},{3,2},{4,5},{5,4},{6,7},{7,6},{8,9},{9,8},{10,11... | collective-permute-start | bytes 3145736 | tf_op jit(solution)/shard_map/ppermute | solution.py:303
  79.0 3.9 %copy-start.2 = (bf16[4,512,128]{2,1,0:T(8,128)(2,1)S(1)}, bf16[4,512,128]{2,1,0:T(8,128)(2,1)}, u32[]{:S(2)}) copy-start(bf16[4,512,128]{2,1,0:T(8,128)(2,1)} %copy-done.1) | copy-start | bytes 1572868
  79.0 3.9 %copy-start.5 = (bf16[128,128]{1,0:T(8,128)(2,1)S(1)}, bf16[128,128]{1,0:T(8,128)(2,1)}, u32[]{:S(2)}) copy-start(bf16[128,128]{1,0:T(8,128)(2,1)} %wout_ref.1) | copy-start | bytes 98308

commit v6 on v5

--- a/solution.py
+++ b/solution.py
@@ -59,18 +59,33 @@
         out_ref[:, :, lane * 128 : (lane + 1) * 128] = part.astype(BF16)
 
 
-def edges_kernel(pair_ref, mask_ref, gains_ref, w_ref, out_ref, scratch):
+def edges_kernel(
+    pair_any, mask_any, gains_any, w_any, out_any, scratch, pair_ref, mask_ref, gains_ref, w_ref, out_ref, sems
+):
     rows, total = mask_ref.shape
     hidden = out_ref.shape[0]
+    arrays = ((pair_any, pair_ref), (mask_any, mask_ref), (gains_any, gains_ref), (w_any, w_ref))
+    copies = [pltpu.make_async_copy(src, dst, sems.at[at]) for at, (src, dst) in enumerate(arrays)]
+    for copy in copies:
+        copy.start()
+    for copy in copies:
+        copy.wait()
     normed = [norm_rows(pair_ref[row], gains_ref[0:1, :]) for row in range(rows)]
-    edges = [dot(w_ref[...], normed[row], 0, 1) for row in range(rows)]
+    edges = [dot(normed[row], w_ref[...], 1, 0) for row in range(rows)]
     for row in range(rows):
         mask = mask_ref[row : row + 1, :].astype(F32)
         for side in range(2):
-            gate = edges[row][2 * side * hidden : (2 * side + 1) * hidden]
-            value = edges[row][(2 * side + 1) * hidden : (2 * side + 2) * hidden]
-            put_rows(scratch, side * rows + row, TILE, mask * sigmoid(gate) * value)
-    fill(out_ref, scratch)
+            gate = edges[row][:, 2 * side * hidden : (2 * side + 1) * hidden]
+            value = edges[row][:, (2 * side + 1) * hidden : (2 * side + 2) * hidden]
+            put_rows(scratch, side * rows + row, TILE, mask * (sigmoid(gate) * value).T)
+    copies = []
+    for lane in range(scratch.shape[0]):
+        here = slice(lane * 128, (lane + 1) * 128)
+        out_ref[:, :, here] = scratch[lane].reshape(hidden, TILE, 128).astype(BF16)
+        copies.append(pltpu.make_async_copy(out_ref.at[:, :, here], out_any.at[:, :, here], sems.at[4 + lane]))
+        copies[lane].start()
+    for copy in copies:
+        copy.wait()
 
 
 def gate_kernel(pair_ref, mask_ref, gains_ref, wg_ref, wb_ref, gate_ref, small_ref):
@@ -156,20 +171,27 @@
     base = first_head[0]
     lane_head = lax.broadcasted_iota(jnp.int32, (1, width), 1) // head_dim
     mine = (lane_head >= base) & (lane_head < base + own)
+    step = total // 4
+    picks = [(lane_head == base + head).astype(BF16) for head in range(own)]
     attended = []
     for row in range(rows):
-        expos, boths = [], []
-        for head in range(own):
-            pick = (lane_head == base + head).astype(BF16)
-            bias = jnp.concatenate([bias_f[head, lane] for lane in range(total // 128)], axis=1)
-            logits = dot(query_ref[row] * pick, key_ref[row], 1, 1) + bias + small_ref[MASK_AT + row : MASK_AT + row + 1, :]
-            top = jnp.max(logits, axis=-1, keepdims=True)
-            expos.append(jnp.exp2(logits - top).astype(BF16))
-            value = value_ref[row]
-            boths.append(
-                jnp.concatenate([value * pick, jnp.broadcast_to(pick, value.shape)], axis=1)
-            )
-        mixed = dot(jnp.concatenate(expos, axis=1), jnp.concatenate(boths, axis=0), 1, 0)
+        value = value_ref[row]
+        both = jnp.concatenate(
+            [jnp.concatenate([value * pick, jnp.broadcast_to(pick, value.shape)], axis=1) for pick in picks],
+            axis=0,
+        )
+        mixed = []
+        for at in range(0, total, step):
+            here = slice(at, at + step)
+            expos = []
+            for head in range(own):
+                bias = jnp.concatenate([bias_f[head, lane, here] for lane in range(total // 128)], axis=1)
+                logits = dot(query_ref[row, here] * picks[head], key_ref[row], 1, 1) + bias
+                logits = logits + small_ref[MASK_AT + row : MASK_AT + row + 1, :]
+                top = jnp.max(logits, axis=-1, keepdims=True)
+                expos.append(jnp.exp2(logits - top).astype(BF16))
+            mixed.append(dot(jnp.concatenate(expos, axis=1), both, 1, 0))
+        mixed = jnp.concatenate(mixed, axis=0)
         share = jnp.where(mine, mixed[:, :width] / mixed[:, width:], 0.0)
         attended.append((gate_ref[row] * share).astype(BF16))
     return attended
@@ -237,9 +259,9 @@
         copy.wait()
 
 
-def call(kernel, out_shape, scratch, n_args, scalars=0, limit=VMEM_LIMIT, out_space=pltpu.VMEM, cost=None):
+def call(kernel, out_shape, scratch, n_args, scalars=0, limit=VMEM_LIMIT, in_space=pltpu.VMEM, out_space=pltpu.VMEM, cost=None):
     specs = [
-        pl.BlockSpec(memory_space=pltpu.SMEM if at < scalars else pltpu.VMEM) for at in range(n_args)
+        pl.BlockSpec(memory_space=pltpu.SMEM if at < scalars else in_space) for at in range(n_args)
     ]
     return pl.pallas_call(
         kernel,
@@ -270,9 +292,17 @@
     tall = pltpu.VMEM((lanes, devices * TILE, 128), F32)
     square = pltpu.VMEM((lanes, total, 128), F32)
     short = pltpu.VMEM((lanes // 2, devices * TILE, 128), F32)
+    inputs = [pair, pair_mask, norm_gains, w_edges]
+    kept = [pltpu.VMEM(array.shape, array.dtype) for array in inputs]
     sides = call(
-        edges_kernel, shape((hidden, TILE, total), BF16), [tall], 4, limit=EDGES_LIMIT
-    )(pair, pair_mask, norm_gains, w_edges)
+        edges_kernel,
+        shape((hidden, TILE, total), BF16),
+        [tall] + kept + [pltpu.VMEM((hidden, TILE, total), BF16), pltpu.SemaphoreType.DMA((4 + lanes,))],
+        4,
+        limit=EDGES_LIMIT,
+        in_space=pl.ANY,
+        out_space=pl.ANY,
+    )(*inputs)
     gate, small = call(
         gate_kernel,
         [shape((rows, total, width), F32), shape((SMALL, total), F32)],

time: 87.4 us -> 87.2 us (level)
  no operation moved by 1% of the time
where the time goes in v6:
time: 87.2 us; the launch traced here: 86.9 us
  blocking collectives  41.5 us (48%)
  waiting for transfers between devices  18 us (21%)
  Pallas kernels  14 us (16%)
  starting transfers between devices  12.4 us (14%)
    all_to_all x2, blocking collectives, exchange(): return lax.all_to_all(array, 'dap', 0, 0, tiled=True)  41.5 us
    all_to_all x1, waiting for transfers between devices, exchange(): return lax.all_to_all(array, 'dap', 0, 0, tiled=True)  18 us
    all_to_all x1, starting transfers between devices, exchange(): return lax.all_to_all(array, 'dap', 0, 0, tiled=True)  11.5 us
    pallas_call x1, Pallas kernels, per_device(): call(functools.partial(other_heads_kernel, head_dim), like, scratch, 10,...  4.01 us
    pallas_call x1, Pallas kernels, per_device(): call(functools.partial(own_heads_kernel, head_dim), [like, like, like, wi...  3.75 us
    pallas_call x1, Pallas kernels, per_device(): call(edges_kernel, shape((hidden, TILE, total), BF16), [tall] + kept + [p...  3.3 us
  transfers between devices with their start and end apart: 2, of which 1 were waited for; matrix products, arithmetic and copies ran while one was open for 0% of the time, Pallas kernels for 5%

profile of v6, /device:TPU:1, one launch (start us, length us, event | category | flops | bytes accessed | tf_op | source)
XLA Modules:
  0.0 86.9 jit_solution(8614646310324097487)
XLA Ops:
  0.0 3.3 %shard_map.91 = bf16[128,8,512]{2,1,0:T(8,128)(2,1)} custom-call(bf16[4,512,128]{2,1,0:T(8,128)(2,1)} %pair_ref.3, s32[4,512]{1,0:T(4,128)} %mask_ref.1, f32[3,128]{1,0:T(4,128)} %gains_ref.1, bf16[128,512]{1,0:T(8,128)(2,1)} %w_any.1), custom_call_target="tpu_custom_call" | custom-call | tf_op jit(solution)/shard_map/pallas_call | solution.py:297
  3.3 0.0 copy-start
  3.3 0.0 copy-start.6
  3.3 0.0 copy-start.7
  3.3 0.0 copy-start.8
  3.4 11.5 %all-to-all-start = ((bf16[128,8,512]{2,1,0:T(8,128)(2,1)}), bf16[128,8,512]{2,1,0:T(8,128)(2,1)S(1)}, u32[]{:S(2)}, u32[]{:S(2)}) async-start(bf16[128,8,512]{2,1,0:T(8,128)(2,1)} %shard_map.91), calls=%async_computation | async-start | bytes 2097152 | tf_op jit(solution)/shard_map/all_to_all | solution.py:278
  14.9 0.0 copy-start.9
  14.9 0.0 copy-done
  14.9 0.0 copy-done.6
  14.9 0.0 copy-done.7
  14.9 0.0 copy-done.8
  14.9 0.6 copy-done.9
  15.6 0.7 shard_map.92
  16.2 18.0 %all-to-all-done.sides_ref = bf16[128,8,512]{2,1,0:T(8,128)(2,1)S(1)} async-done(((bf16[128,8,512]{2,1,0:T(8,128)(2,1)}), bf16[128,8,512]{2,1,0:T(8,128)(2,1)S(1)}, u32[]{:S(2)}, u32[]{:S(2)}) %all-to-all-start) | async-done | bytes 1048608 | tf_op jit(solution)/shard_map/all_to_all | solution.py:278
  34.2 0.9 %shard_map.93 = bf16[128,8,256]{2,1,0:T(8,128)(2,1)S(1)} custom-call(bf16[128,8,512]{2,1,0:T(8,128)(2,1)S(1)} %all-to-all-done.sides_ref), custom_call_target="tpu_custom_call" | custom-call | tf_op jit(solution)/shard_map/pallas_call | solution.py:319
  35.2 0.0 copy-start.4
  35.2 17.9 %all_to_all.15.prod_ref = bf16[128,8,256]{2,1,0:T(8,128)(2,1)S(1)} all-to-all(bf16[128,8,256]{2,1,0:T(8,128)(2,1)S(1)} %shard_map.93), channel_id=1, replica_groups=mesh['dap'=128] {'dap'}, dimensions={0} | all-to-all | bytes 1048576 | tf_op jit(solution)/shard_map/all_to_all | solution.py:278
  53.0 0.0 copy-done.4
  53.0 1.3 %shard_map.94 = (bf16[4,512,128]{2,1,0:T(8,128)(2,1)S(1)}, bf16[4,512,128]{2,1,0:T(8,128)(2,1)S(1)}, bf16[128,8,512]{2,1,0:T(8,128)(2,1)S(1)}) custom-call(bf16[128,8,256]{2,1,0:T(8,128)(2,1)S(1)} %all_to_all.15.prod_ref, bf16[4,512,128]{2,1,0:T(8,128)(2,1)S(1)} %copy-done, f32[4,512,128]{2,1,0:T(8,128)S(1)} %get-tuple-element.21.gate_ref, ...), custom_call_target="tpu_custom_call" | custom-call | tf_op jit(solution)/shard_map/pallas_call | solution.py:325
  54.4 0.0 copy-start.1
  54.4 0.0 copy-start.3
  54.4 23.7 %all_to_all.16.bias_ref = bf16[128,8,512]{2,1,0:T(8,128)(2,1)S(1)} all-to-all(bf16[128,8,512]{2,1,0:T(8,128)(2,1)S(1)} %get-tuple-element.24), channel_id=1, replica_groups=mesh['dap'=128] {'dap'}, dimensions={0} | all-to-all | bytes 2097152 | tf_op jit(solution)/shard_map/all_to_all | solution.py:278
  78.1 0.0 copy-done.1
  78.1 0.9 %collective-permute-start = (bf16[128,8,512]{2,1,0:T(8,128)(2,1)S(1)}, bf16[128,8,512]{2,1,0:T(8,128)(2,1)S(1)}, u32[]{:S(2)}, u32[]{:S(2)}) collective-permute-start(bf16[128,8,512]{2,1,0:T(8,128)(2,1)S(1)} %all_to_all.16.bias_ref), channel_id=1, source_target_pairs={{0,1},{1,0},{2,3},{3,2},{4,5},{5,4},{6,7},{7,6},{8,9},{9,8},{10,11... | collective-permute-start | bytes 3145736 | tf_op jit(solution)/shard_map/ppermute | solution.py:333
  78.9 0.0 copy-done.3
  78.9 0.0 copy-start.2
  78.9 0.0 copy-start.5
  78.9 3.7 %shard_map.95 = (bf16[4,512,128]{2,1,0:T(8,128)(2,1)S(1)}, bf16[4,512,128]{2,1,0:T(8,128)(2,1)S(1)}, bf16[4,512,128]{2,1,0:T(8,128)(2,1)S(1)}, f32[4,512,128]{2,1,0:T(8,128)S(1)}, bf16[4,512,128]{2,1,0:T(8,128)(2,1)S(1)}) custom-call(s32[1]{0:T(128)} %bitcast.1.first_head, bf16[4,512,128]{2,1,0:T(8,128)(2,1)S(1)} %get-tuple-element.23.normed_ref, ...), custom_call_target="tpu_custom_call" | custom-call | tf_op jit(solution)/shard_map/pallas_call | solution.py:338
  82.7 0.0 collective-permute-done.bias_ref
  82.7 0.0 copy-done.2
  82.7 0.0 copy-done.5
  82.7 4.0 %shard_map.96 = bf16[4,512,128]{2,1,0:T(8,128)(2,1)} custom-call(s32[1]{0:T(128)} %bitcast.first_head, bf16[4,512,128]{2,1,0:T(8,128)(2,1)S(1)} %get-tuple-element.25.query_ref, bf16[4,512,128]{2,1,0:T(8,128)(2,1)S(1)} %get-tuple-element.26.key_ref, bf16[4,512,128]{2,1,0:T(8,128)(2,1)S(1)} %get-tuple-element.27.value_ref, ...), custom_call_target="tpu_custom_call" | custom-call | tf_op jit(solution)/shard_map/pallas_call | solution.py:346
Async XLA Ops:
  3.3 11.6 %copy-start = (bf16[4,512,128]{2,1,0:T(8,128)(2,1)S(1)}, bf16[4,512,128]{2,1,0:T(8,128)(2,1)}, u32[]{:S(2)}) copy-start(bf16[4,512,128]{2,1,0:T(8,128)(2,1)} %pair_ref.3) | copy-start | bytes 1572868
  3.3 11.6 %copy-start.6 = (s32[4,512]{1,0:T(4,128)S(1)}, s32[4,512]{1,0:T(4,128)}, u32[]{:S(2)}) copy-start(s32[4,512]{1,0:T(4,128)} %mask_ref.1) | copy-start | bytes 24580
  3.3 11.6 %copy-start.7 = (bf16[128,128]{1,0:T(8,128)(2,1)S(1)}, bf16[128,128]{1,0:T(8,128)(2,1)}, u32[]{:S(2)}) copy-start(bf16[128,128]{1,0:T(8,128)(2,1)} %wg_ref.1) | copy-start | bytes 98308
  3.3 11.6 %copy-start.8 = (f32[3,128]{1,0:T(4,128)S(1)}, f32[3,128]{1,0:T(4,128)}, u32[]{:S(2)}) copy-start(f32[3,128]{1,0:T(4,128)} %gains_ref.1) | copy-start | bytes 4612
  3.4 30.9 %all-to-all-start = ((bf16[128,8,512]{2,1,0:T(8,128)(2,1)}), bf16[128,8,512]{2,1,0:T(8,128)(2,1)S(1)}, u32[]{:S(2)}, u32[]{:S(2)}) async-start(bf16[128,8,512]{2,1,0:T(8,128)(2,1)} %shard_map.91), calls=%async_computation | async-start | bytes 2097152 | tf_op jit(solution)/shard_map/all_to_all | solution.py:278
  14.9 0.7 copy-start.9
  35.2 17.9 %copy-start.4 = (bf16[128,128]{1,0:T(8,128)(2,1)S(1)}, bf16[128,128]{1,0:T(8,128)(2,1)}, u32[]{:S(2)}) copy-start(bf16[128,128]{1,0:T(8,128)(2,1)} %wo_ref.1) | copy-start | bytes 98308
  54.4 23.7 %copy-start.1 = (bf16[4,512,128]{2,1,0:T(8,128)(2,1)}, bf16[4,512,128]{2,1,0:T(8,128)(2,1)S(1)}, u32[]{:S(2)}) copy-start(bf16[4,512,128]{2,1,0:T(8,128)(2,1)S(1)} %get-tuple-element.29.mid_ref) | copy-start | bytes 1572868
  54.4 24.6 %copy-start.3 = (bf16[128,512]{1,0:T(8,128)(2,1)S(1)}, bf16[128,512]{1,0:T(8,128)(2,1)}, u32[]{:S(2)}) copy-start(bf16[128,512]{1,0:T(8,128)(2,1)} %win_ref.1) | copy-start | bytes 393220
  78.1 4.6 %collective-permute-start = (bf16[128,8,512]{2,1,0:T(8,128)(2,1)S(1)}, bf16[128,8,512]{2,1,0:T(8,128)(2,1)S(1)}, u32[]{:S(2)}, u32[]{:S(2)}) collective-permute-start(bf16[128,8,512]{2,1,0:T(8,128)(2,1)S(1)} %all_to_all.16.bias_ref), channel_id=1, source_target_pairs={{0,1},{1,0},{2,3},{3,2},{4,5},{5,4},{6,7},{7,6},{8,9},{9,8},{10,11... | collective-permute-start | bytes 3145736 | tf_op jit(solution)/shard_map/ppermute | solution.py:333
  78.9 3.8 %copy-start.2 = (bf16[4,512,128]{2,1,0:T(8,128)(2,1)S(1)}, bf16[4,512,128]{2,1,0:T(8,128)(2,1)}, u32[]{:S(2)}) copy-start(bf16[4,512,128]{2,1,0:T(8,128)(2,1)} %copy-done.1) | copy-start | bytes 1572868
  78.9 3.8 %copy-start.5 = (bf16[128,128]{1,0:T(8,128)(2,1)S(1)}, bf16[128,128]{1,0:T(8,128)(2,1)}, u32[]{:S(2)}) copy-start(bf16[128,128]{1,0:T(8,128)(2,1)} %wout_ref.1) | copy-start | bytes 98308

commit v7 on v6

--- a/solution.py
+++ b/solution.py
@@ -50,12 +50,12 @@
 def spill(scratch, values):
     for lane in range(scratch.shape[0]):
         part = values[:, :, lane * 128 : (lane + 1) * 128].astype(F32)
-        scratch[lane] = part.reshape(scratch.shape[1], 128)
+        scratch[lane, 0 : values.shape[0] * TILE, :] = part.reshape(values.shape[0] * TILE, 128)
 
 
 def fill(out_ref, scratch):
     for lane in range(scratch.shape[0]):
-        part = scratch[lane].reshape(out_ref.shape[0], TILE, 128)
+        part = scratch[lane, 0 : out_ref.shape[0] * TILE, :].reshape(out_ref.shape[0], TILE, 128)
         out_ref[:, :, lane * 128 : (lane + 1) * 128] = part.astype(BF16)
 
 
@@ -81,7 +81,7 @@
     copies = []
     for lane in range(scratch.shape[0]):
         here = slice(lane * 128, (lane + 1) * 128)
-        out_ref[:, :, here] = scratch[lane].reshape(hidden, TILE, 128).astype(BF16)
+        out_ref[:, :, here] = scratch[lane, 0 : hidden * TILE, :].reshape(hidden, TILE, 128).astype(BF16)
         copies.append(pltpu.make_async_copy(out_ref.at[:, :, here], out_any.at[:, :, here], sems.at[4 + lane]))
         copies[lane].start()
     for copy in copies:
@@ -106,7 +106,7 @@
     spill(scratch, sides_ref[...])
     for row in range(rows):
         put_rows(right_ref, row, rows, get_rows(scratch, rows + row, devices, TILE))
-    right = jnp.concatenate([right_ref[lane] for lane in range(total // 128)], axis=1).astype(BF16)
+    right = jnp.concatenate([right_ref[lane, 0:total, :] for lane in range(total // 128)], axis=1).astype(BF16)
     left = [get_rows(scratch, row, devices, TILE).astype(BF16) for row in range(rows)]
     product = dot(jnp.concatenate(left, axis=0), right, 1, 1)
     for row in range(rows):
@@ -289,9 +289,9 @@
     devices = total // rows
     lanes = total // 128
     shape = jax.ShapeDtypeStruct
-    tall = pltpu.VMEM((lanes, devices * TILE, 128), F32)
-    square = pltpu.VMEM((lanes, total, 128), F32)
-    short = pltpu.VMEM((lanes // 2, devices * TILE, 128), F32)
+    tall = pltpu.VMEM((lanes, (devices + 1) * TILE, 128), F32)
+    square = pltpu.VMEM((lanes, total + TILE, 128), F32)
+    short = pltpu.VMEM((lanes // 2, (devices + 1) * TILE, 128), F32)
     inputs = [pair, pair_mask, norm_gains, w_edges]
     kept = [pltpu.VMEM(array.shape, array.dtype) for array in inputs]
     sides = call(
@@ -334,7 +334,7 @@
     core = lax.rem(lax.axis_index("dap"), 2)
     mine_first = jnp.reshape(core * own, (1,))
     other_first = jnp.reshape((1 - core) * own, (1,))
-    scratch = [tall, pltpu.VMEM((own, lanes, total, 128), F32)]
+    scratch = [tall, pltpu.VMEM((own, lanes, total + TILE, 128), F32)]
     query, key, value, att_gate, part = call(
         functools.partial(own_heads_kernel, head_dim),
         [like, like, like, wide, like],

time: 87.2 us -> 87.2 us (level)
  no operation moved by 1% of the time
where the time goes in v7:
time: 87.2 us; the launch traced here: 86.9 us
  blocking collectives  41.5 us (48%)
  waiting for transfers between devices  18 us (21%)
  Pallas kernels  14 us (16%)
  starting transfers between devices  12.4 us (14%)
    all_to_all x2, blocking collectives, exchange(): return lax.all_to_all(array, 'dap', 0, 0, tiled=True)  41.5 us
    all_to_all x1, waiting for transfers between devices, exchange(): return lax.all_to_all(array, 'dap', 0, 0, tiled=True)  18 us
    all_to_all x1, starting transfers between devices, exchange(): return lax.all_to_all(array, 'dap', 0, 0, tiled=True)  11.5 us
    pallas_call x1, Pallas kernels, per_device(): call(functools.partial(other_heads_kernel, head_dim), like, scratch, 10,...  4.01 us
    pallas_call x1, Pallas kernels, per_device(): call(functools.partial(own_heads_kernel, head_dim), [like, like, like, wi...  3.73 us
    pallas_call x1, Pallas kernels, per_device(): call(edges_kernel, shape((hidden, TILE, total), BF16), [tall] + kept + [p...  3.3 us
  transfers between devices with their start and end apart: 2, of which 1 were waited for; matrix products, arithmetic and copies ran while one was open for 0% of the time, Pallas kernels for 5%

profile of v7, /device:TPU:1, one launch (start us, length us, event | category | flops | bytes accessed | tf_op | source)
XLA Modules:
  0.0 86.9 jit_solution(12377612346219582299)
XLA Ops:
  0.0 3.3 %shard_map.91 = bf16[128,8,512]{2,1,0:T(8,128)(2,1)} custom-call(bf16[4,512,128]{2,1,0:T(8,128)(2,1)} %pair_ref.3, s32[4,512]{1,0:T(4,128)} %mask_ref.1, f32[3,128]{1,0:T(4,128)} %gains_ref.1, bf16[128,512]{1,0:T(8,128)(2,1)} %w_any.1), custom_call_target="tpu_custom_call" | custom-call | tf_op jit(solution)/shard_map/pallas_call | solution.py:297
  3.3 0.0 copy-start
  3.3 0.0 copy-start.6
  3.3 0.0 copy-start.7
  3.3 0.0 copy-start.8
  3.4 11.5 %all-to-all-start = ((bf16[128,8,512]{2,1,0:T(8,128)(2,1)}), bf16[128,8,512]{2,1,0:T(8,128)(2,1)S(1)}, u32[]{:S(2)}, u32[]{:S(2)}) async-start(bf16[128,8,512]{2,1,0:T(8,128)(2,1)} %shard_map.91), calls=%async_computation | async-start | bytes 2097152 | tf_op jit(solution)/shard_map/all_to_all | solution.py:278
  14.9 0.0 copy-start.9
  14.9 0.0 copy-done
  14.9 0.0 copy-done.6
  14.9 0.0 copy-done.7
  14.9 0.0 copy-done.8
  14.9 0.6 copy-done.9
  15.6 0.7 shard_map.92
  16.2 18.0 %all-to-all-done.sides_ref = bf16[128,8,512]{2,1,0:T(8,128)(2,1)S(1)} async-done(((bf16[128,8,512]{2,1,0:T(8,128)(2,1)}), bf16[128,8,512]{2,1,0:T(8,128)(2,1)S(1)}, u32[]{:S(2)}, u32[]{:S(2)}) %all-to-all-start) | async-done | bytes 1048608 | tf_op jit(solution)/shard_map/all_to_all | solution.py:278
  34.2 0.9 %shard_map.93 = bf16[128,8,256]{2,1,0:T(8,128)(2,1)S(1)} custom-call(bf16[128,8,512]{2,1,0:T(8,128)(2,1)S(1)} %all-to-all-done.sides_ref), custom_call_target="tpu_custom_call" | custom-call | tf_op jit(solution)/shard_map/pallas_call | solution.py:319
  35.1 0.0 copy-start.4
  35.1 17.9 %all_to_all.15.prod_ref = bf16[128,8,256]{2,1,0:T(8,128)(2,1)S(1)} all-to-all(bf16[128,8,256]{2,1,0:T(8,128)(2,1)S(1)} %shard_map.93), channel_id=1, replica_groups=mesh['dap'=128] {'dap'}, dimensions={0} | all-to-all | bytes 1048576 | tf_op jit(solution)/shard_map/all_to_all | solution.py:278
  53.0 0.0 copy-done.4
  53.0 1.3 %shard_map.94 = (bf16[4,512,128]{2,1,0:T(8,128)(2,1)S(1)}, bf16[4,512,128]{2,1,0:T(8,128)(2,1)S(1)}, bf16[128,8,512]{2,1,0:T(8,128)(2,1)S(1)}) custom-call(bf16[128,8,256]{2,1,0:T(8,128)(2,1)S(1)} %all_to_all.15.prod_ref, bf16[4,512,128]{2,1,0:T(8,128)(2,1)S(1)} %copy-done, f32[4,512,128]{2,1,0:T(8,128)S(1)} %get-tuple-element.21.gate_ref, ...), custom_call_target="tpu_custom_call" | custom-call | tf_op jit(solution)/shard_map/pallas_call | solution.py:325
  54.3 0.0 copy-start.1
  54.4 0.0 copy-start.3
  54.4 23.7 %all_to_all.16.bias_ref = bf16[128,8,512]{2,1,0:T(8,128)(2,1)S(1)} all-to-all(bf16[128,8,512]{2,1,0:T(8,128)(2,1)S(1)} %get-tuple-element.24), channel_id=1, replica_groups=mesh['dap'=128] {'dap'}, dimensions={0} | all-to-all | bytes 2097152 | tf_op jit(solution)/shard_map/all_to_all | solution.py:278
  78.0 0.0 copy-done.1
  78.0 0.9 %collective-permute-start = (bf16[128,8,512]{2,1,0:T(8,128)(2,1)S(1)}, bf16[128,8,512]{2,1,0:T(8,128)(2,1)S(1)}, u32[]{:S(2)}, u32[]{:S(2)}) collective-permute-start(bf16[128,8,512]{2,1,0:T(8,128)(2,1)S(1)} %all_to_all.16.bias_ref), channel_id=1, source_target_pairs={{0,1},{1,0},{2,3},{3,2},{4,5},{5,4},{6,7},{7,6},{8,9},{9,8},{10,11... | collective-permute-start | bytes 3145736 | tf_op jit(solution)/shard_map/ppermute | solution.py:333
  78.9 0.0 copy-done.3
  78.9 0.0 copy-start.2
  78.9 0.0 copy-start.5
  78.9 3.7 %shard_map.95 = (bf16[4,512,128]{2,1,0:T(8,128)(2,1)S(1)}, bf16[4,512,128]{2,1,0:T(8,128)(2,1)S(1)}, bf16[4,512,128]{2,1,0:T(8,128)(2,1)S(1)}, f32[4,512,128]{2,1,0:T(8,128)S(1)}, bf16[4,512,128]{2,1,0:T(8,128)(2,1)S(1)}) custom-call(s32[1]{0:T(128)} %bitcast.1.first_head, bf16[4,512,128]{2,1,0:T(8,128)(2,1)S(1)} %get-tuple-element.23.normed_ref, ...), custom_call_target="tpu_custom_call" | custom-call | tf_op jit(solution)/shard_map/pallas_call | solution.py:338
  82.7 0.0 collective-permute-done.bias_ref
  82.7 0.0 copy-done.2
  82.7 0.0 copy-done.5
  82.7 4.0 %shard_map.96 = bf16[4,512,128]{2,1,0:T(8,128)(2,1)} custom-call(s32[1]{0:T(128)} %bitcast.first_head, bf16[4,512,128]{2,1,0:T(8,128)(2,1)S(1)} %get-tuple-element.25.query_ref, bf16[4,512,128]{2,1,0:T(8,128)(2,1)S(1)} %get-tuple-element.26.key_ref, bf16[4,512,128]{2,1,0:T(8,128)(2,1)S(1)} %get-tuple-element.27.value_ref, ...), custom_call_target="tpu_custom_call" | custom-call | tf_op jit(solution)/shard_map/pallas_call | solution.py:346
Async XLA Ops:
  3.3 11.6 %copy-start = (bf16[4,512,128]{2,1,0:T(8,128)(2,1)S(1)}, bf16[4,512,128]{2,1,0:T(8,128)(2,1)}, u32[]{:S(2)}) copy-start(bf16[4,512,128]{2,1,0:T(8,128)(2,1)} %pair_ref.3) | copy-start | bytes 1572868
  3.3 11.6 %copy-start.6 = (s32[4,512]{1,0:T(4,128)S(1)}, s32[4,512]{1,0:T(4,128)}, u32[]{:S(2)}) copy-start(s32[4,512]{1,0:T(4,128)} %mask_ref.1) | copy-start | bytes 24580
  3.3 11.6 %copy-start.7 = (bf16[128,128]{1,0:T(8,128)(2,1)S(1)}, bf16[128,128]{1,0:T(8,128)(2,1)}, u32[]{:S(2)}) copy-start(bf16[128,128]{1,0:T(8,128)(2,1)} %wg_ref.1) | copy-start | bytes 98308
  3.3 11.6 %copy-start.8 = (f32[3,128]{1,0:T(4,128)S(1)}, f32[3,128]{1,0:T(4,128)}, u32[]{:S(2)}) copy-start(f32[3,128]{1,0:T(4,128)} %gains_ref.1) | copy-start | bytes 4612
  3.4 30.9 %all-to-all-start = ((bf16[128,8,512]{2,1,0:T(8,128)(2,1)}), bf16[128,8,512]{2,1,0:T(8,128)(2,1)S(1)}, u32[]{:S(2)}, u32[]{:S(2)}) async-start(bf16[128,8,512]{2,1,0:T(8,128)(2,1)} %shard_map.91), calls=%async_computation | async-start | bytes 2097152 | tf_op jit(solution)/shard_map/all_to_all | solution.py:278
  14.9 0.7 copy-start.9
  35.1 17.9 %copy-start.4 = (bf16[128,128]{1,0:T(8,128)(2,1)S(1)}, bf16[128,128]{1,0:T(8,128)(2,1)}, u32[]{:S(2)}) copy-start(bf16[128,128]{1,0:T(8,128)(2,1)} %wo_ref.1) | copy-start | bytes 98308
  54.3 23.7 %copy-start.1 = (bf16[4,512,128]{2,1,0:T(8,128)(2,1)}, bf16[4,512,128]{2,1,0:T(8,128)(2,1)S(1)}, u32[]{:S(2)}) copy-start(bf16[4,512,128]{2,1,0:T(8,128)(2,1)S(1)} %get-tuple-element.29.mid_ref) | copy-start | bytes 1572868
  54.4 24.6 %copy-start.3 = (bf16[128,512]{1,0:T(8,128)(2,1)S(1)}, bf16[128,512]{1,0:T(8,128)(2,1)}, u32[]{:S(2)}) copy-start(bf16[128,512]{1,0:T(8,128)(2,1)} %win_ref.1) | copy-start | bytes 393220
  78.0 4.6 %collective-permute-start = (bf16[128,8,512]{2,1,0:T(8,128)(2,1)S(1)}, bf16[128,8,512]{2,1,0:T(8,128)(2,1)S(1)}, u32[]{:S(2)}, u32[]{:S(2)}) collective-permute-start(bf16[128,8,512]{2,1,0:T(8,128)(2,1)S(1)} %all_to_all.16.bias_ref), channel_id=1, source_target_pairs={{0,1},{1,0},{2,3},{3,2},{4,5},{5,4},{6,7},{7,6},{8,9},{9,8},{10,11... | collective-permute-start | bytes 3145736 | tf_op jit(solution)/shard_map/ppermute | solution.py:333
  78.9 3.8 %copy-start.2 = (bf16[4,512,128]{2,1,0:T(8,128)(2,1)S(1)}, bf16[4,512,128]{2,1,0:T(8,128)(2,1)}, u32[]{:S(2)}) copy-start(bf16[4,512,128]{2,1,0:T(8,128)(2,1)} %copy-done.1) | copy-start | bytes 1572868
  78.9 3.8 %copy-start.5 = (bf16[128,128]{1,0:T(8,128)(2,1)S(1)}, bf16[128,128]{1,0:T(8,128)(2,1)}, u32[]{:S(2)}) copy-start(bf16[128,128]{1,0:T(8,128)(2,1)} %wout_ref.1) | copy-start | bytes 98308

commit v8 on v4

--- a/solution.py
+++ b/solution.py
@@ -25,15 +25,19 @@
     return 0.5 + 0.5 * jnp.tanh(0.5 * x)
 
 
-def norm_rows(values, gain):
+def norm_rows(values, gain, mats):
     size = values.shape[-1]
+    centered = dot(values, mats[0:size], 1, 0)
+    var = dot((centered * centered).astype(BF16), mats[size : 2 * size], 1, 0)
+    return (centered * lax.rsqrt(var + 1e-05) * gain).astype(BF16)
+
+
+def mats_kernel(out_ref):
+    size = out_ref.shape[1]
     row = lax.broadcasted_iota(jnp.int32, (size, size), 0)
     col = lax.broadcasted_iota(jnp.int32, (size, size), 1)
-    centering = ((row == col).astype(F32) - 1.0 / size).astype(BF16)
-    average = jnp.full((size, size), 1.0 / size, BF16)
-    centered = dot(values, centering, 1, 0)
-    var = dot((centered * centered).astype(BF16), average, 1, 0)
-    return (centered * lax.rsqrt(var + 1e-05) * gain).astype(BF16)
+    out_ref[0:size, :] = ((row == col).astype(F32) - 1.0 / size).astype(BF16)
+    out_ref[size : 2 * size, :] = jnp.full((size, size), 1.0 / size, BF16)
 
 
 def put_rows(scratch, start, stride, values):
@@ -50,23 +54,26 @@
 def spill(scratch, values):
     for lane in range(scratch.shape[0]):
         part = values[:, :, lane * 128 : (lane + 1) * 128].astype(F32)
-        scratch[lane] = part.reshape(scratch.shape[1], 128)
+        scratch[lane, 0 : values.shape[0] * TILE, :] = part.reshape(values.shape[0] * TILE, 128)
 
 
 def fill(out_ref, scratch):
     for lane in range(scratch.shape[0]):
-        part = scratch[lane].reshape(out_ref.shape[0], TILE, 128)
+        part = scratch[lane, 0 : out_ref.shape[0] * TILE, :].reshape(out_ref.shape[0], TILE, 128)
         out_ref[:, :, lane * 128 : (lane + 1) * 128] = part.astype(BF16)
 
 
-def edges_kernel(pair_ref, mask_ref, gains_ref, w_ref, wg_ref, wb_ref, out_ref, gate_ref, small_ref, scratch):
+def edges_kernel(
+    mats_ref, pair_ref, mask_ref, gains_ref, w_ref, wg_ref, wb_ref, out_ref, gate_ref, small_ref, scratch
+):
     rows, total = mask_ref.shape
+    hidden = out_ref.shape[0]
     width = gains_ref.shape[1]
     small_ref[MASK_AT : MASK_AT + rows, :] = (1000000000.0 * LOG2E) * (mask_ref[...].astype(F32) - 1.0)
     small_ref[GAIN_AT : GAIN_AT + 3, 0:width] = gains_ref[...]
     small_ref[BIAS_AT : BIAS_AT + wb_ref.shape[0], 0:width] = wb_ref[...].astype(F32)
-    hidden = out_ref.shape[0]
-    normed = [norm_rows(pair_ref[row], gains_ref[0:1, :]) for row in range(rows)]
+    mats = mats_ref[...]
+    normed = [norm_rows(pair_ref[row], gains_ref[0:1, :], mats) for row in range(rows)]
     edges = [dot(w_ref[...], normed[row], 0, 1) for row in range(rows)]
     for row in range(rows):
         gate_ref[row] = sigmoid(dot(normed[row], wg_ref[...], 1, 0))
@@ -86,7 +93,7 @@
     spill(scratch, sides_ref[...])
     for row in range(rows):
         put_rows(right_ref, row, rows, get_rows(scratch, rows + row, devices, TILE))
-    right = jnp.concatenate([right_ref[lane] for lane in range(total // 128)], axis=1).astype(BF16)
+    right = jnp.concatenate([right_ref[lane, 0:total, :] for lane in range(total // 128)], axis=1).astype(BF16)
     left = [get_rows(scratch, row, devices, TILE).astype(BF16) for row in range(rows)]
     product = dot(jnp.concatenate(left, axis=0), right, 1, 1)
     for row in range(rows):
@@ -96,6 +103,7 @@
 
 
 def middle_kernel(
+    mats_ref,
     prod_ref,
     pair_ref,
     gate_ref,
@@ -127,7 +135,7 @@
     mid_normed = []
     for row in range(rows):
         mid_ref[row] = mid[row]
-        mid_normed.append(norm_rows(mid[row], small_ref[GAIN_AT + 2 : GAIN_AT + 3, 0:width]))
+        mid_normed.append(norm_rows(mid[row], small_ref[GAIN_AT + 2 : GAIN_AT + 3, 0:width], mats_ref[...]))
         normed_ref[row] = mid_normed[row]
     bias = [dot(wb, mid_normed[row], 1, 1) for row in range(rows)]
     for row in range(rows):
@@ -151,20 +159,27 @@
     base = first_head[0]
     lane_head = lax.broadcasted_iota(jnp.int32, (1, width), 1) // head_dim
     mine = (lane_head >= base) & (lane_head < base + own)
+    step = total // 4
+    picks = [(lane_head == base + head).astype(BF16) for head in range(own)]
     attended = []
     for row in range(rows):
-        expos, boths = [], []
-        for head in range(own):
-            pick = (lane_head == base + head).astype(BF16)
-            bias = jnp.concatenate([bias_f[head, lane] for lane in range(total // 128)], axis=1)
-            logits = dot(query_ref[row] * pick, key_ref[row], 1, 1) + bias + small_ref[MASK_AT + row : MASK_AT + row + 1, :]
-            top = jnp.max(logits, axis=-1, keepdims=True)
-            expos.append(jnp.exp2(logits - top).astype(BF16))
-            value = value_ref[row]
-            boths.append(
-                jnp.concatenate([value * pick, jnp.broadcast_to(pick, value.shape)], axis=1)
-            )
-        mixed = dot(jnp.concatenate(expos, axis=1), jnp.concatenate(boths, axis=0), 1, 0)
+        value = value_ref[row]
+        both = jnp.concatenate(
+            [jnp.concatenate([value * pick, jnp.broadcast_to(pick, value.shape)], axis=1) for pick in picks],
+            axis=0,
+        )
+        mixed = []
+        for at in range(0, total, step):
+            here = slice(at, at + step)
+            expos = []
+            for head in range(own):
+                bias = jnp.concatenate([bias_f[head, lane, here] for lane in range(total // 128)], axis=1)
+                logits = dot(query_ref[row, here] * picks[head], key_ref[row], 1, 1) + bias
+                logits = logits + small_ref[MASK_AT + row : MASK_AT + row + 1, :]
+                top = jnp.max(logits, axis=-1, keepdims=True)
+                expos.append(jnp.exp2(logits - top).astype(BF16))
+            mixed.append(dot(jnp.concatenate(expos, axis=1), both, 1, 0))
+        mixed = jnp.concatenate(mixed, axis=0)
         share = jnp.where(mine, mixed[:, :width] / mixed[:, width:], 0.0)
         attended.append((gate_ref[row] * share).astype(BF16))
     return attended
@@ -232,9 +247,9 @@
         copy.wait()
 
 
-def call(kernel, out_shape, scratch, n_args, scalars=0, limit=VMEM_LIMIT, out_space=pltpu.VMEM):
+def call(kernel, out_shape, scratch, n_args, scalars=0, limit=VMEM_LIMIT, in_space=pltpu.VMEM, out_space=pltpu.VMEM, cost=None):
     specs = [
-        pl.BlockSpec(memory_space=pltpu.SMEM if at < scalars else pltpu.VMEM) for at in range(n_args)
+        pl.BlockSpec(memory_space=pltpu.SMEM if at < scalars else in_space) for at in range(n_args)
     ]
     return pl.pallas_call(
         kernel,
@@ -243,6 +258,7 @@
         out_shape=out_shape,
         scratch_shapes=scratch,
         compiler_params=pltpu.CompilerParams(vmem_limit_bytes=limit),
+        cost_estimate=cost,
     )
 
 
@@ -261,9 +277,16 @@
     devices = total // rows
     lanes = total // 128
     shape = jax.ShapeDtypeStruct
-    tall = pltpu.VMEM((lanes, devices * TILE, 128), F32)
-    square = pltpu.VMEM((lanes, total, 128), F32)
-    short = pltpu.VMEM((lanes // 2, devices * TILE, 128), F32)
+    tall = pltpu.VMEM((lanes, (devices + 1) * TILE, 128), F32)
+    square = pltpu.VMEM((lanes, total + TILE, 128), F32)
+    short = pltpu.VMEM((lanes // 2, (devices + 1) * TILE, 128), F32)
+    mats = call(
+        mats_kernel,
+        shape((2 * width, width), BF16),
+        [],
+        0,
+        cost=pl.CostEstimate(flops=1 << 31, bytes_accessed=8 << 20, transcendentals=0),
+    )()
     sides, gate, small = call(
         edges_kernel,
         [
@@ -272,9 +295,8 @@
             shape((SMALL, total), F32),
         ],
         [tall],
-        6,
-        limit=EDGES_LIMIT,
-    )(pair, pair_mask, norm_gains, w_edges, w_tri_gate, w_tri_bias.T)
+        7,
+    )(mats, pair, pair_mask, norm_gains, w_edges, w_tri_gate, w_tri_bias.T)
     sides = exchange(sides)
     product = call(
         product_kernel, shape((devices, TILE, total // 2), BF16), [tall, square, short], 1
@@ -286,15 +308,15 @@
         middle_kernel,
         [like, like, shape((devices, TILE, total), BF16)],
         [short, pltpu.VMEM((2 * TILE, total), F32)],
-        5,
-    )(product, pair, gate, small, w_tri_out)
+        6,
+    )(mats, product, pair, gate, small, w_tri_out)
     mine = exchange(bias)
     swap = [(d, d ^ 1) for d in range(devices)]
     other = lax.ppermute(mine, "dap", swap)
     core = lax.rem(lax.axis_index("dap"), 2)
     mine_first = jnp.reshape(core * own, (1,))
     other_first = jnp.reshape((1 - core) * own, (1,))
-    scratch = [tall, pltpu.VMEM((own, lanes, total, 128), F32)]
+    scratch = [tall, pltpu.VMEM((own, lanes, total + TILE, 128), F32)]
     query, key, value, att_gate, part = call(
         functools.partial(own_heads_kernel, head_dim),
         [like, like, like, wide, like],

time: 88.1 us -> 86.6 us (0.983)
  Pallas kernels: 14.3 us -> 11.9 us
  local copies, waits for them, and re-layouts: 0.03 us -> 1.12 us
    pallas_call x1, Pallas kernels: 3.85 us -> 1.46 us  [per_device(): call(edges_kernel, [shape((hidden, TILE, total), BF16), shape((rows, tota...]
    unnamed x12 -> x18, local copies, waits for them, and re-layouts: 0.03 us -> 1.12 us
where the time goes in v8:
time: 86.6 us; the launch traced here: 86.4 us
  blocking collectives  72.2 us (83%)
  Pallas kernels  11.9 us (14%)
  local copies, waits for them, and re-layouts  1.12 us (1%)
  starting transfers between devices  0.87 us (1%)
    all_to_all x3, blocking collectives, exchange(): return lax.all_to_all(array, 'dap', 0, 0, tiled=True)  72.2 us
    pallas_call x1, Pallas kernels, per_device(): call(functools.partial(other_heads_kernel, head_dim), like, scratch, 10,...  4.28 us
    pallas_call x1, Pallas kernels, per_device(): call(functools.partial(own_heads_kernel, head_dim), [like, like, like, wi...  3.97 us
  transfers between devices with their start and end apart: 1, of which 0 were waited for; matrix products, arithmetic and copies ran while one was open for 0% of the time, Pallas kernels for 5%

profile of v8, /device:TPU:1, one launch (start us, length us, event | category | flops | bytes accessed | tf_op | source)
XLA Modules:
  0.0 86.4 jit_solution(15718633270139124881)
XLA Ops:
  0.0 0.0 copy-start.6
  0.0 0.0 copy-start.2
  0.0 0.0 copy-start.5
  0.0 0.0 copy-start
  0.0 0.0 copy-start.7
  0.1 0.0 copy-start.8
  0.1 0.6 copy-done.6
  0.7 0.2 copy-done.2
  0.9 0.0 copy-done.5
  0.9 0.2 copy-done
  1.1 0.0 copy-done.7
  1.2 0.0 copy-done.8
  1.2 1.5 %shard_map.92 = (bf16[128,8,512]{2,1,0:T(8,128)(2,1)S(1)}, f32[4,512,128]{2,1,0:T(8,128)S(1)}, f32[24,512]{1,0:T(8,128)S(1)}) custom-call(bf16[256,128]{1,0:T(8,128)(2,1)S(1)} %shard_map.91.mats_ref, bf16[4,512,128]{2,1,0:T(8,128)(2,1)S(1)} %copy-done, s32[4,512]{1,0:T(4,128)S(1)} %copy-done.6, f32[3,128]{1,0:T(4,128)S(1)} %copy-done.7, ...), custom_call_target="tpu_custom_call" | custom-call | tf_op jit(solution)/shard_map/pallas_call | solution.py:290
  2.6 30.6 %all_to_all.15.sides_ref = bf16[128,8,512]{2,1,0:T(8,128)(2,1)S(1)} all-to-all(bf16[128,8,512]{2,1,0:T(8,128)(2,1)S(1)} %get-tuple-element.16), channel_id=1, replica_groups=mesh['dap'=128] {'dap'}, dimensions={0} | all-to-all | bytes 2097152 | tf_op jit(solution)/shard_map/all_to_all | solution.py:266
  33.3 0.9 %shard_map.93 = bf16[128,8,256]{2,1,0:T(8,128)(2,1)S(1)} custom-call(bf16[128,8,512]{2,1,0:T(8,128)(2,1)S(1)} %all_to_all.15.sides_ref), custom_call_target="tpu_custom_call" | custom-call | tf_op jit(solution)/shard_map/pallas_call | solution.py:301
  34.2 0.0 copy-start.3
  34.2 17.9 %all_to_all.16.prod_ref = bf16[128,8,256]{2,1,0:T(8,128)(2,1)S(1)} all-to-all(bf16[128,8,256]{2,1,0:T(8,128)(2,1)S(1)} %shard_map.93), channel_id=1, replica_groups=mesh['dap'=128] {'dap'}, dimensions={0} | all-to-all | bytes 1048576 | tf_op jit(solution)/shard_map/all_to_all | solution.py:266
  52.1 0.0 copy-done.3
  52.1 1.3 %shard_map.94 = (bf16[4,512,128]{2,1,0:T(8,128)(2,1)S(1)}, bf16[4,512,128]{2,1,0:T(8,128)(2,1)S(1)}, bf16[128,8,512]{2,1,0:T(8,128)(2,1)S(1)}) custom-call(bf16[256,128]{1,0:T(8,128)(2,1)S(1)} %shard_map.91.mats_ref, bf16[128,8,256]{2,1,0:T(8,128)(2,1)S(1)} %all_to_all.16.prod_ref, bf16[4,512,128]{2,1,0:T(8,128)(2,1)S(1)} %copy-done, ...), custom_call_target="tpu_custom_call" | custom-call | tf_op jit(solution)/shard_map/pallas_call | solution.py:307
  53.4 0.0 copy-start.1
  53.4 23.7 %all_to_all.17.bias_ref = bf16[128,8,512]{2,1,0:T(8,128)(2,1)S(1)} all-to-all(bf16[128,8,512]{2,1,0:T(8,128)(2,1)S(1)} %get-tuple-element.20), channel_id=1, replica_groups=mesh['dap'=128] {'dap'}, dimensions={0} | all-to-all | bytes 2097152 | tf_op jit(solution)/shard_map/all_to_all | solution.py:266
  77.1 0.9 %collective-permute-start = (bf16[128,8,512]{2,1,0:T(8,128)(2,1)S(1)}, bf16[128,8,512]{2,1,0:T(8,128)(2,1)S(1)}, u32[]{:S(2)}, u32[]{:S(2)}) collective-permute-start(bf16[128,8,512]{2,1,0:T(8,128)(2,1)S(1)} %all_to_all.17.bias_ref), channel_id=1, source_target_pairs={{0,1},{1,0},{2,3},{3,2},{4,5},{5,4},{6,7},{7,6},{8,9},{9,8},{10,11... | collective-permute-start | bytes 3145736 | tf_op jit(solution)/shard_map/ppermute | solution.py:315
  77.9 0.0 copy-done.1
  77.9 0.0 copy-start.4
  77.9 4.0 %shard_map.95 = (bf16[4,512,128]{2,1,0:T(8,128)(2,1)S(1)}, bf16[4,512,128]{2,1,0:T(8,128)(2,1)S(1)}, bf16[4,512,128]{2,1,0:T(8,128)(2,1)S(1)}, f32[4,512,128]{2,1,0:T(8,128)S(1)}, bf16[4,512,128]{2,1,0:T(8,128)(2,1)S(1)}) custom-call(s32[1]{0:T(128)} %bitcast.1.first_head, bf16[4,512,128]{2,1,0:T(8,128)(2,1)S(1)} %get-tuple-element.19.normed_ref, ...), custom_call_target="tpu_custom_call" | custom-call | tf_op jit(solution)/shard_map/pallas_call | solution.py:320
  81.9 0.0 collective-permute-done.bias_ref
  81.9 0.0 copy-done.4
  81.9 4.3 %shard_map.96 = bf16[4,512,128]{2,1,0:T(8,128)(2,1)} custom-call(s32[1]{0:T(128)} %bitcast.first_head, bf16[4,512,128]{2,1,0:T(8,128)(2,1)S(1)} %get-tuple-element.21.query_ref, bf16[4,512,128]{2,1,0:T(8,128)(2,1)S(1)} %get-tuple-element.22.key_ref, bf16[4,512,128]{2,1,0:T(8,128)(2,1)S(1)} %get-tuple-element.23.value_ref, ...), custom_call_target="tpu_custom_call" | custom-call | tf_op jit(solution)/shard_map/pallas_call | solution.py:328
  (1 shorter events, 0.0 us)
Async XLA Ops:
  0.0 0.7 copy-start.6
  0.0 0.9 %copy-start.2 = (bf16[128,512]{1,0:T(8,128)(2,1)S(1)}, bf16[128,512]{1,0:T(8,128)(2,1)}, u32[]{:S(2)}) copy-start(bf16[128,512]{1,0:T(8,128)(2,1)} %w_ref.1) | copy-start | bytes 393220
  0.0 0.9 %copy-start.5 = (bf16[128,128]{1,0:T(8,128)(2,1)S(1)}, bf16[128,128]{1,0:T(8,128)(2,1)}, u32[]{:S(2)}) copy-start(bf16[128,128]{1,0:T(8,128)(2,1)} %wg_ref.1) | copy-start | bytes 98308
  0.0 1.1 %copy-start = (bf16[4,512,128]{2,1,0:T(8,128)(2,1)S(1)}, bf16[4,512,128]{2,1,0:T(8,128)(2,1)}, u32[]{:S(2)}) copy-start(bf16[4,512,128]{2,1,0:T(8,128)(2,1)} %pair_ref.3) | copy-start | bytes 1572868
  0.0 1.1 %copy-start.7 = (f32[3,128]{1,0:T(4,128)S(1)}, f32[3,128]{1,0:T(4,128)}, u32[]{:S(2)}) copy-start(f32[3,128]{1,0:T(4,128)} %gains_ref.1) | copy-start | bytes 4612
  0.1 1.1 %copy-start.8 = (bf16[128,4]{0,1:T(4,128)(2,1)S(1)}, bf16[128,4]{0,1:T(4,128)(2,1)}, u32[]{:S(2)}) copy-start(bf16[128,4]{0,1:T(4,128)(2,1)} %param.16) | copy-start | bytes 3076
  34.2 17.9 %copy-start.3 = (bf16[128,128]{1,0:T(8,128)(2,1)S(1)}, bf16[128,128]{1,0:T(8,128)(2,1)}, u32[]{:S(2)}) copy-start(bf16[128,128]{1,0:T(8,128)(2,1)} %wo_ref.1) | copy-start | bytes 98308
  53.4 24.6 %copy-start.1 = (bf16[128,512]{1,0:T(8,128)(2,1)S(1)}, bf16[128,512]{1,0:T(8,128)(2,1)}, u32[]{:S(2)}) copy-start(bf16[128,512]{1,0:T(8,128)(2,1)} %win_ref.1) | copy-start | bytes 393220
  77.1 4.9 %collective-permute-start = (bf16[128,8,512]{2,1,0:T(8,128)(2,1)S(1)}, bf16[128,8,512]{2,1,0:T(8,128)(2,1)S(1)}, u32[]{:S(2)}, u32[]{:S(2)}) collective-permute-start(bf16[128,8,512]{2,1,0:T(8,128)(2,1)S(1)} %all_to_all.17.bias_ref), channel_id=1, source_target_pairs={{0,1},{1,0},{2,3},{3,2},{4,5},{5,4},{6,7},{7,6},{8,9},{9,8},{10,11... | collective-permute-start | bytes 3145736 | tf_op jit(solution)/shard_map/ppermute | solution.py:315
  77.9 4.0 %copy-start.4 = (bf16[128,128]{1,0:T(8,128)(2,1)S(1)}, bf16[128,128]{1,0:T(8,128)(2,1)}, u32[]{:S(2)}) copy-start(bf16[128,128]{1,0:T(8,128)(2,1)} %wout_ref.1) | copy-start | bytes 98308

commit v9 on v8

--- a/solution.py
+++ b/solution.py
@@ -137,7 +137,7 @@
         mid_ref[row] = mid[row]
         mid_normed.append(norm_rows(mid[row], small_ref[GAIN_AT + 2 : GAIN_AT + 3, 0:width], mats_ref[...]))
         normed_ref[row] = mid_normed[row]
-    bias = [dot(wb, mid_normed[row], 1, 1) for row in range(rows)]
+    bias = [dot(wb, mid_normed[row], 1, 1) * LOG2E for row in range(rows)]
     for row in range(rows):
         for head in range(heads):
             bias_f[head * rows + row : head * rows + row + 1, :] = bias[row][head : head + 1, :]
@@ -154,7 +154,7 @@
     spill(scratch, bias_ref[...])
     for head in range(own):
         for row in range(rows):
-            values = get_rows(scratch, head * rows + row, devices, TILE) * LOG2E
+            values = get_rows(scratch, head * rows + row, devices, TILE)
             put_rows(bias_f.at[head], row, rows, values)
     base = first_head[0]
     lane_head = lax.broadcasted_iota(jnp.int32, (1, width), 1) // head_dim

time: 86.6 us -> 86.5 us (level)
  no operation moved by 1% of the time
where the time goes in v9:
time: 86.5 us; the launch traced here: 86.3 us
  blocking collectives  72.2 us (83%)
  Pallas kernels  11.9 us (14%)
  local copies, waits for them, and re-layouts  1.12 us (1%)
  starting transfers between devices  0.87 us (1%)
    all_to_all x3, blocking collectives, exchange(): return lax.all_to_all(array, 'dap', 0, 0, tiled=True)  72.2 us
    pallas_call x1, Pallas kernels, per_device(): call(functools.partial(other_heads_kernel, head_dim), like, scratch, 10,...  4.2 us
    pallas_call x1, Pallas kernels, per_device(): call(functools.partial(own_heads_kernel, head_dim), [like, like, like, wi...  3.97 us
  transfers between devices with their start and end apart: 1, of which 0 were waited for; matrix products, arithmetic and copies ran while one was open for 0% of the time, Pallas kernels for 5%

profile of v9, /device:TPU:1, one launch (start us, length us, event | category | flops | bytes accessed | tf_op | source)
XLA Modules:
  0.0 86.3 jit_solution(1924962368633480968)
XLA Ops:
  0.0 0.0 copy-start.6
  0.0 0.0 copy-start.2
  0.0 0.0 copy-start.5
  0.0 0.0 copy-start
  0.0 0.0 copy-start.7
  0.1 0.0 copy-start.8
  0.1 0.6 copy-done.6
  0.7 0.2 copy-done.2
  0.9 0.0 copy-done.5
  0.9 0.2 copy-done
  1.1 0.0 copy-done.7
  1.2 0.0 copy-done.8
  1.2 1.5 %shard_map.92 = (bf16[128,8,512]{2,1,0:T(8,128)(2,1)S(1)}, f32[4,512,128]{2,1,0:T(8,128)S(1)}, f32[24,512]{1,0:T(8,128)S(1)}) custom-call(bf16[256,128]{1,0:T(8,128)(2,1)S(1)} %shard_map.91.mats_ref, bf16[4,512,128]{2,1,0:T(8,128)(2,1)S(1)} %copy-done, s32[4,512]{1,0:T(4,128)S(1)} %copy-done.6, f32[3,128]{1,0:T(4,128)S(1)} %copy-done.7, ...), custom_call_target="tpu_custom_call" | custom-call | tf_op jit(solution)/shard_map/pallas_call | solution.py:290
  2.6 30.6 %all_to_all.15.sides_ref = bf16[128,8,512]{2,1,0:T(8,128)(2,1)S(1)} all-to-all(bf16[128,8,512]{2,1,0:T(8,128)(2,1)S(1)} %get-tuple-element.16), channel_id=1, replica_groups=mesh['dap'=128] {'dap'}, dimensions={0} | all-to-all | bytes 2097152 | tf_op jit(solution)/shard_map/all_to_all | solution.py:266
  33.3 0.9 %shard_map.93 = bf16[128,8,256]{2,1,0:T(8,128)(2,1)S(1)} custom-call(bf16[128,8,512]{2,1,0:T(8,128)(2,1)S(1)} %all_to_all.15.sides_ref), custom_call_target="tpu_custom_call" | custom-call | tf_op jit(solution)/shard_map/pallas_call | solution.py:301
  34.2 0.0 copy-start.3
  34.2 17.9 %all_to_all.16.prod_ref = bf16[128,8,256]{2,1,0:T(8,128)(2,1)S(1)} all-to-all(bf16[128,8,256]{2,1,0:T(8,128)(2,1)S(1)} %shard_map.93), channel_id=1, replica_groups=mesh['dap'=128] {'dap'}, dimensions={0} | all-to-all | bytes 1048576 | tf_op jit(solution)/shard_map/all_to_all | solution.py:266
  52.1 0.0 copy-done.3
  52.1 1.3 %shard_map.94 = (bf16[4,512,128]{2,1,0:T(8,128)(2,1)S(1)}, bf16[4,512,128]{2,1,0:T(8,128)(2,1)S(1)}, bf16[128,8,512]{2,1,0:T(8,128)(2,1)S(1)}) custom-call(bf16[256,128]{1,0:T(8,128)(2,1)S(1)} %shard_map.91.mats_ref, bf16[128,8,256]{2,1,0:T(8,128)(2,1)S(1)} %all_to_all.16.prod_ref, bf16[4,512,128]{2,1,0:T(8,128)(2,1)S(1)} %copy-done, ...), custom_call_target="tpu_custom_call" | custom-call | tf_op jit(solution)/shard_map/pallas_call | solution.py:307
  53.4 0.0 copy-start.1
  53.4 23.7 %all_to_all.17.bias_ref = bf16[128,8,512]{2,1,0:T(8,128)(2,1)S(1)} all-to-all(bf16[128,8,512]{2,1,0:T(8,128)(2,1)S(1)} %get-tuple-element.20), channel_id=1, replica_groups=mesh['dap'=128] {'dap'}, dimensions={0} | all-to-all | bytes 2097152 | tf_op jit(solution)/shard_map/all_to_all | solution.py:266
  77.1 0.9 %collective-permute-start = (bf16[128,8,512]{2,1,0:T(8,128)(2,1)S(1)}, bf16[128,8,512]{2,1,0:T(8,128)(2,1)S(1)}, u32[]{:S(2)}, u32[]{:S(2)}) collective-permute-start(bf16[128,8,512]{2,1,0:T(8,128)(2,1)S(1)} %all_to_all.17.bias_ref), channel_id=1, source_target_pairs={{0,1},{1,0},{2,3},{3,2},{4,5},{5,4},{6,7},{7,6},{8,9},{9,8},{10,11... | collective-permute-start | bytes 3145736 | tf_op jit(solution)/shard_map/ppermute | solution.py:315
  77.9 0.0 copy-done.1
  77.9 0.0 copy-start.4
  77.9 4.0 %shard_map.95 = (bf16[4,512,128]{2,1,0:T(8,128)(2,1)S(1)}, bf16[4,512,128]{2,1,0:T(8,128)(2,1)S(1)}, bf16[4,512,128]{2,1,0:T(8,128)(2,1)S(1)}, f32[4,512,128]{2,1,0:T(8,128)S(1)}, bf16[4,512,128]{2,1,0:T(8,128)(2,1)S(1)}) custom-call(s32[1]{0:T(128)} %bitcast.1.first_head, bf16[4,512,128]{2,1,0:T(8,128)(2,1)S(1)} %get-tuple-element.19.normed_ref, ...), custom_call_target="tpu_custom_call" | custom-call | tf_op jit(solution)/shard_map/pallas_call | solution.py:320
  81.9 0.0 collective-permute-done.bias_ref
  81.9 0.0 copy-done.4
  81.9 4.2 %shard_map.96 = bf16[4,512,128]{2,1,0:T(8,128)(2,1)} custom-call(s32[1]{0:T(128)} %bitcast.first_head, bf16[4,512,128]{2,1,0:T(8,128)(2,1)S(1)} %get-tuple-element.21.query_ref, bf16[4,512,128]{2,1,0:T(8,128)(2,1)S(1)} %get-tuple-element.22.key_ref, bf16[4,512,128]{2,1,0:T(8,128)(2,1)S(1)} %get-tuple-element.23.value_ref, ...), custom_call_target="tpu_custom_call" | custom-call | tf_op jit(solution)/shard_map/pallas_call | solution.py:328
  (1 shorter events, 0.0 us)
Async XLA Ops:
  0.0 0.7 copy-start.6
  0.0 0.9 %copy-start.2 = (bf16[128,512]{1,0:T(8,128)(2,1)S(1)}, bf16[128,512]{1,0:T(8,128)(2,1)}, u32[]{:S(2)}) copy-start(bf16[128,512]{1,0:T(8,128)(2,1)} %w_ref.1) | copy-start | bytes 393220
  0.0 0.9 %copy-start.5 = (bf16[128,128]{1,0:T(8,128)(2,1)S(1)}, bf16[128,128]{1,0:T(8,128)(2,1)}, u32[]{:S(2)}) copy-start(bf16[128,128]{1,0:T(8,128)(2,1)} %wg_ref.1) | copy-start | bytes 98308
  0.0 1.1 %copy-start = (bf16[4,512,128]{2,1,0:T(8,128)(2,1)S(1)}, bf16[4,512,128]{2,1,0:T(8,128)(2,1)}, u32[]{:S(2)}) copy-start(bf16[4,512,128]{2,1,0:T(8,128)(2,1)} %pair_ref.3) | copy-start | bytes 1572868
  0.0 1.1 %copy-start.7 = (f32[3,128]{1,0:T(4,128)S(1)}, f32[3,128]{1,0:T(4,128)}, u32[]{:S(2)}) copy-start(f32[3,128]{1,0:T(4,128)} %gains_ref.1) | copy-start | bytes 4612
  0.1 1.1 %copy-start.8 = (bf16[128,4]{0,1:T(4,128)(2,1)S(1)}, bf16[128,4]{0,1:T(4,128)(2,1)}, u32[]{:S(2)}) copy-start(bf16[128,4]{0,1:T(4,128)(2,1)} %param.16) | copy-start | bytes 3076
  34.2 17.9 %copy-start.3 = (bf16[128,128]{1,0:T(8,128)(2,1)S(1)}, bf16[128,128]{1,0:T(8,128)(2,1)}, u32[]{:S(2)}) copy-start(bf16[128,128]{1,0:T(8,128)(2,1)} %wo_ref.1) | copy-start | bytes 98308
  53.4 24.6 %copy-start.1 = (bf16[128,512]{1,0:T(8,128)(2,1)S(1)}, bf16[128,512]{1,0:T(8,128)(2,1)}, u32[]{:S(2)}) copy-start(bf16[128,512]{1,0:T(8,128)(2,1)} %win_ref.1) | copy-start | bytes 393220
  77.1 4.9 %collective-permute-start = (bf16[128,8,512]{2,1,0:T(8,128)(2,1)S(1)}, bf16[128,8,512]{2,1,0:T(8,128)(2,1)S(1)}, u32[]{:S(2)}, u32[]{:S(2)}) collective-permute-start(bf16[128,8,512]{2,1,0:T(8,128)(2,1)S(1)} %all_to_all.17.bias_ref), channel_id=1, source_target_pairs={{0,1},{1,0},{2,3},{3,2},{4,5},{5,4},{6,7},{7,6},{8,9},{9,8},{10,11... | collective-permute-start | bytes 3145736 | tf_op jit(solution)/shard_map/ppermute | solution.py:315
  77.9 4.0 %copy-start.4 = (bf16[128,128]{1,0:T(8,128)(2,1)S(1)}, bf16[128,128]{1,0:T(8,128)(2,1)}, u32[]{:S(2)}) copy-start(bf16[128,128]{1,0:T(8,128)(2,1)} %wout_ref.1) | copy-start | bytes 98308
